TPU v7x, 512 devices: a whole 4x8x8 slice. The times are simulated.
512 devices in a mesh: dom: 64 (over y, z), tp: 8 (over x, core).
Axes of the slice: x: 4, y: 8, z: 8, core: 2. Of those that a mesh axis runs over, the one named last changes fastest.
Arguments:
- query: bfloat16 [128, 3584], P('dom', 'tp'), may hold values from -200 to 200
- new_kv: bfloat16 [128, 2, 512], P('dom'), may hold values from -8 to 8
- cache: bfloat16 [128, 2, 4096, 512], P('dom', None, 'tp'), may hold values from -8 to 8
- lengths: int32 [128], P('dom'), may hold values from 1024 to 4095, as said below
- prior_logw: float32 [128], P('dom'), may hold values from -250 to 250
- ancestors: int32 [128], replicated, may hold values from 0 to 127, as said below
- w_reward: bfloat16 [3584], replicated, may hold values from -0.09375 to 0.09375
Outputs:
- attn_out: bfloat16 [128, 3584], P('dom', 'tp')
- log_weight: float32 [128], P('dom')
- new_cache: bfloat16 [128, 2, 4096, 512], P('dom', None, 'tp')
Inputs may be any that keep to these rules, and one draw needn't show every extreme that they name: `ancestors`: the ancestor of particle i belongs to a device d' with |d' - i // 2| <= 2, each distance up to 2 occurring in every draw; from any other device a device takes the cache of at most one particle. `lengths`: cache positions below it hold the particle's keys and values.
All inputs are finite; a program needn't handle non-finite values.
Results may differ from a plain program's by a relative error of at most 0.004.
Values may be sent and summed in bfloat16 or wider, within the bound.
No kernel may reach another device: no remote copies, remote signals or barrier semaphores. Data moves between devices by JAX's collectives and lax.ppermute only.
A program may use at most 64 MiB of HBM per device.

v0:
```python
import jax
import jax.numpy as jnp
from jax import lax
from jax.sharding import PartitionSpec as P

HQ = 28
KVH = 4
HD = 128
SPAN = 512
REACH = 2


MASKED = -1e30
EPSILON = 1e-06


def merged(part, axis, combine):
    gathered = jax.tree.map(lambda a: lax.all_gather(a, axis), part)

    def take(source):
        return jax.tree.map(lambda a: lax.dynamic_index_in_dim(a, source, 0, False), gathered)

    return lax.fori_loop(
        1, lax.axis_size(axis), lambda source, state: combine(state, take(source)), take(0)
    )


def shifted(value, axis, by):
    devices = lax.axis_size(axis)
    pairs = [(i, i + by) for i in range(devices) if 0 <= i + by < devices]
    return lax.ppermute(value, axis, pairs)


def combine_partial(earlier, later):
    joined = jnp.maximum(earlier[0], later[0])
    first_scale = jnp.exp(earlier[0] - joined)
    second_scale = jnp.exp(later[0] - joined)
    total = earlier[1] * first_scale + later[1] * second_scale
    summed = earlier[2] * first_scale[..., None] + later[2] * second_scale[..., None]
    return (joined, total, summed)


def local(query, new_kv, cache, lengths, prior_logw, ancestors, w_reward):
    count = cache.shape[0]
    local_len = cache.shape[2]
    group = HQ // KVH
    scale = HD ** (-0.5)
    blocks = local_len // SPAN
    dom_index = lax.axis_index("dom")
    tp_index = lax.axis_index("tp")
    first = dom_index * count
    heads = lax.all_gather(query, "tp", axis=1, tiled=True).reshape(count, KVH, group, HD)
    position = tp_index * local_len + jnp.arange(local_len, dtype=jnp.int32)
    grown = jnp.where(
        position[None, None, :, None] == lengths[:, None, None, None], new_kv[:, :, None, :], cache
    )
    keys = cache[:, 0].reshape(count, local_len, KVH, HD)
    values = cache[:, 1].reshape(count, blocks, SPAN, KVH, HD)
    scores = jnp.einsum("pgqd,ptgd->pgqt", heads, keys, preferred_element_type=jnp.float32) * scale
    valid = position[None, :] < lengths[:, None]
    scores = jnp.where(valid[:, None, None, :], scores, MASKED).reshape(
        count, KVH, group, blocks, SPAN
    )
    valid_blocks = valid.reshape(count, 1, 1, blocks, SPAN)
    block_max = jnp.max(scores, axis=4)
    expo = jnp.where(valid_blocks, jnp.exp(scores - block_max[..., None]), 0.0)
    block_sum = jnp.sum(expo, axis=4)
    block_acc = jnp.einsum(
        "pgqbt,pbtgd->pgqbd", expo.astype(jnp.bfloat16), values, preferred_element_type=jnp.float32
    )
    local_max = jnp.max(block_max, axis=3)
    factor = jnp.exp(block_max - local_max[..., None])
    local_sum = jnp.sum(factor * block_sum, axis=3)
    local_acc = jnp.sum(factor[..., None] * block_acc, axis=3)
    joined_max, joined_sum, joined_acc = merged(
        (local_max, local_sum, local_acc), "tp", combine_partial
    )
    own_key = new_kv[:, 0].reshape(count, KVH, HD)
    own_value = new_kv[:, 1].astype(jnp.float32).reshape(count, KVH, 1, HD)
    own_score = (
        jnp.einsum("pgqd,pgd->pgq", heads, own_key, preferred_element_type=jnp.float32) * scale
    )
    top = jnp.maximum(joined_max, own_score)
    kept = jnp.exp(joined_max - top)
    own_factor = jnp.exp(own_score - top)
    numer = kept[..., None] * joined_acc + own_factor[..., None] * own_value
    denom = kept * joined_sum + own_factor
    attended = (numer / denom[..., None]).reshape(count, HQ * HD)
    columns = query.shape[1]
    attn_part = lax.dynamic_slice_in_dim(attended, tp_index * columns, columns, 1).astype(
        jnp.bfloat16
    )
    spread = jnp.sqrt(jnp.mean(attended * attended, axis=1, keepdims=True) + EPSILON)
    reward = jnp.sum(w_reward.astype(jnp.float32)[None, :] * attended / spread, axis=1)
    logits = prior_logw + reward
    peak = lax.pmax(jnp.max(logits), "dom")
    total = lax.psum(jnp.sum(jnp.exp(logits - peak)), "dom")
    log_weight = logits - (peak + jnp.log(total))
    mine = lax.dynamic_slice_in_dim(ancestors, first, count)
    source = mine // count
    slot = mine % count
    new_cache = jnp.take(grown, slot, axis=0)
    offsets = [step for step in range(-REACH, REACH + 1) if step != 0]
    for offset in offsets:
        arrived = shifted(grown, "dom", -offset)
        picked = jnp.take(arrived, slot, axis=0)
        new_cache = jnp.where(
            (source == dom_index + offset)[:, None, None, None], picked, new_cache
        )
    return (attn_part, log_weight, new_cache)


def solution(mesh):
    in_specs = (
        P("dom", "tp"),
        P("dom", None, None),
        P("dom", None, "tp", None),
        P("dom"),
        P("dom"),
        P(),
        P(),
    )
    out_specs = (P("dom", "tp"), P("dom"), P("dom", None, "tp", None))
    return jax.shard_map(local, mesh=mesh, in_specs=in_specs, out_specs=out_specs, check_vma=False)
```

profile of v0, /device:TPU:6, one launch (start us, length us, event | category | flops | bytes accessed | tf_op | source)
XLA Modules:
  0.0 456.6 jit_solution(1902905758520067575)
XLA Ops:
  0.6 0.7 broadcast_compare_fusion
  1.4 1.9 broadcast_select_fusion
  3.3 1.3 collective-permute-start
  4.6 1.3 collective-permute-start.1
  5.9 6.2 %collective-permute-start.2 = (bf16[2,2,512,512]{3,2,1,0:T(8,128)(2,1)S(1)}, bf16[2,2,512,512]{3,2,1,0:T(8,128)(2,1)}, u32[]{:S(2)}, u32[]{:S(2)}) collective-permute-start(bf16[2,2,512,512]{3,2,1,0:T(8,128)(2,1)S(1)} %broadcast_select_fusion), channel_id=1, source_target_pairs={{0,8},{8,16},{16,24},{24,32},{32,40},{40,48},{48,56},{56,64},{64,7... | collective-permute-start | bytes 6291464 | tf_op jit(solution)/shard_map/ppermute | solution.py:31
  12.1 6.8 %collective-permute-start.3 = (bf16[2,2,512,512]{3,2,1,0:T(8,128)(2,1)S(1)}, bf16[2,2,512,512]{3,2,1,0:T(8,128)(2,1)}, u32[]{:S(2)}, u32[]{:S(2)}) collective-permute-start(bf16[2,2,512,512]{3,2,1,0:T(8,128)(2,1)S(1)} %broadcast_select_fusion), channel_id=1, source_target_pairs={{0,16},{8,24},{16,32},{24,40},{32,48},{40,56},{48,64},{56,72},{64,... | collective-permute-start | bytes 6291464 | tf_op jit(solution)/shard_map/ppermute | solution.py:31
  18.9 1.5 fusion.28
  20.4 1.5 copy.28
  21.9 0.0 copy-done.4
  22.0 12.0 %all-gather.3 = bf16[8,448,2]{1,2,0:T(2,128)(2,1)S(1)} all-gather(bf16[1,448,2]{1,2,0:T(2,128)(2,1)S(1)} %bitcast.70), channel_id=1, replica_groups=mesh['dom'=64,'tp'=8] {'tp'}, dimensions={0}, use_global_device_ids=true | all-gather | bytes 16128 | tf_op jit(solution)/shard_map/all_gather | solution.py:52
  34.0 0.1 reshape.263
  34.1 0.1 fusion.19
  34.2 0.3 fusion.29
  34.6 13.3 %all-gather = f32[16,4,7]{2,1,0:T(4,128)S(1)} all-gather(f32[2,4,7]{2,1,0:T(4,128)S(1)} %get-tuple-element.231), channel_id=2, replica_groups=mesh['dom'=64,'tp'=8] {'tp'}, dimensions={0}, use_global_device_ids=true | all-gather | bytes 2016 | tf_op jit(solution)/shard_map/all_gather | solution.py:18
  47.9 0.2 fusion.11
  48.1 1.5 copy.29
  49.6 0.0 copy-start.5
  49.6 0.0 copy-start.6
  49.6 0.4 fusion.9
  50.1 12.8 %all-gather.1 = f32[16,4,7,1,128]{4,1,3,2,0:T(4,128)S(1)} all-gather(f32[2,4,7,1,128]{4,1,3,2,0:T(4,128)S(1)} %copy.20), channel_id=3, replica_groups=mesh['dom'=64,'tp'=8] {'tp'}, dimensions={0}, use_global_device_ids=true | all-gather | bytes 258048 | tf_op jit(solution)/shard_map/all_gather | solution.py:18
  62.9 12.8 %all-gather.2 = f32[16,4,7]{2,1,0:T(4,128)S(1)} all-gather(f32[2,4,7]{2,1,0:T(4,128)S(1)} %bitcast.67), channel_id=4, replica_groups=mesh['dom'=64,'tp'=8] {'tp'}, dimensions={0}, use_global_device_ids=true | all-gather | bytes 2016 | tf_op jit(solution)/shard_map/all_gather | solution.py:18
  75.7 1.1 while.19
  75.8 0.1 fusion.37
  75.9 0.1 fusion.37
  76.1 0.1 fusion.37
  76.3 0.1 fusion.37
  76.4 0.1 fusion.37
  76.6 0.1 fusion.37
  76.8 0.1 fusion.37
  76.9 0.2 multiply_reduce_fusion
  77.1 0.2 fusion.16
  77.3 0.6 fusion.25
  77.9 214.0 %pmax.7 = f32[]{:T(128)} all-reduce(f32[]{:T(128)} %get-tuple-element.215), channel_id=1, replica_groups=mesh['dom'=64,'tp'=8] {'dom'}, use_global_device_ids=true, to_apply=%region_7.8 | all-reduce | flops 1 | bytes 8 | tf_op jit(solution)/shard_map/pmax | solution.py:96
  291.9 1.2 exponential_reduce_fusion
  293.2 138.6 %psum.7 = f32[]{:T(128)} all-reduce(f32[]{:T(128)} %exponential_reduce_fusion), channel_id=1, replica_groups=mesh['dom'=64,'tp'=8] {'dom'}, use_global_device_ids=true, to_apply=%region_9.10 | all-reduce | flops 1 | bytes 8 | tf_op jit(solution)/shard_map/psum | solution.py:97
  431.8 0.1 broadcast_compare_fusion.5
  431.9 2.0 gather_fusion.4
  435.3 0.7 dynamic-slice_convert_fusion
  435.9 0.5 broadcast_subtract_fusion
  436.4 0.0 collective-permute-done
  436.4 3.6 gather_fusion
  440.0 0.0 collective-permute-done.1
  440.0 3.7 gather_fusion.1
  443.7 0.0 collective-permute-done.2
  443.7 3.6 gather_fusion.2
  447.3 0.0 collective-permute-done.3
  447.3 3.7 gather_fusion.3
  451.0 5.6 %fusion.6 = bf16[2,2,512,512]{3,2,1,0:T(8,128)(2,1)} fusion(bf16[2,2,512,512]{3,2,1,0:T(8,128)(2,1)S(1)} %copy-done.1, bf16[2,2,512,512]{3,2,1,0:T(8,128)(2,1)} %gather_fusion.3, bf16[2,2,512,512]{3,2,1,0:T(8,128)(2,1)} %gather_fusion.2, bf16[2,2,512,512]{3,2,1,0:T(8,128)(2,1)} %gather_fusion.1, bf16[2,2,512,512]{3,2,1,0:T(8,128)(2,1)} %gather_fusion, ...), kind=kLoop, calls=%fused_computation.18 | loop fusion | flops 9437184 | bytes 12582922 | tf_op jit(solution)/shard_map/jit(_where)/select_n | solution.py:107
  (41 shorter events, 0.4 us)
Async XLA Ops:
  1.4 17.6 %copy-start = (bf16[2,2,512,512]{3,2,1,0:T(8,128)(2,1)S(1)}, bf16[2,2,512,512]{3,2,1,0:T(8,128)(2,1)}, u32[]{:S(2)}) copy-start(bf16[2,2,512,512]{3,2,1,0:T(8,128)(2,1)} %param.13) | copy-start | bytes 6291460
  3.3 433.1 %collective-permute-start = (bf16[2,2,512,512]{3,2,1,0:T(8,128)(2,1)S(1)}, bf16[2,2,512,512]{3,2,1,0:T(8,128)(2,1)}, u32[]{:S(2)}, u32[]{:S(2)}) collective-permute-start(bf16[2,2,512,512]{3,2,1,0:T(8,128)(2,1)S(1)} %broadcast_select_fusion), channel_id=1, source_target_pairs={{16,0},{24,8},{32,16},{40,24},{48,32},{56,40},{64,48},{72,56},{80,... | collective-permute-start | bytes 6291464 | tf_op jit(solution)/shard_map/ppermute | solution.py:31
  4.6 435.4 %collective-permute-start.1 = (bf16[2,2,512,512]{3,2,1,0:T(8,128)(2,1)S(1)}, bf16[2,2,512,512]{3,2,1,0:T(8,128)(2,1)}, u32[]{:S(2)}, u32[]{:S(2)}) collective-permute-start(bf16[2,2,512,512]{3,2,1,0:T(8,128)(2,1)S(1)} %broadcast_select_fusion), channel_id=1, source_target_pairs={{8,0},{16,8},{24,16},{32,24},{40,32},{48,40},{56,48},{64,56},{72,6... | collective-permute-start | bytes 6291464 | tf_op jit(solution)/shard_map/ppermute | solution.py:31
  5.9 437.8 %collective-permute-start.2 = (bf16[2,2,512,512]{3,2,1,0:T(8,128)(2,1)S(1)}, bf16[2,2,512,512]{3,2,1,0:T(8,128)(2,1)}, u32[]{:S(2)}, u32[]{:S(2)}) collective-permute-start(bf16[2,2,512,512]{3,2,1,0:T(8,128)(2,1)S(1)} %broadcast_select_fusion), channel_id=1, source_target_pairs={{0,8},{8,16},{16,24},{24,32},{32,40},{40,48},{48,56},{56,64},{64,7... | collective-permute-start | bytes 6291464 | tf_op jit(solution)/shard_map/ppermute | solution.py:31
  12.1 435.2 %collective-permute-start.3 = (bf16[2,2,512,512]{3,2,1,0:T(8,128)(2,1)S(1)}, bf16[2,2,512,512]{3,2,1,0:T(8,128)(2,1)}, u32[]{:S(2)}, u32[]{:S(2)}) collective-permute-start(bf16[2,2,512,512]{3,2,1,0:T(8,128)(2,1)S(1)} %broadcast_select_fusion), channel_id=1, source_target_pairs={{0,16},{8,24},{16,32},{24,40},{32,48},{40,56},{48,64},{56,72},{64,... | collective-permute-start | bytes 6291464 | tf_op jit(solution)/shard_map/ppermute | solution.py:31
  20.4 1.5 copy-start.4
  20.4 13.7 %copy-start.2 = (bf16[2,2,512]{2,1,0:T(2,128)(2,1)S(1)}, bf16[2,2,512]{2,1,0:T(2,128)(2,1)}, u32[]{:S(2)}) copy-start(bf16[2,2,512]{2,1,0:T(2,128)(2,1)} %param.12) | copy-start | bytes 12292
  48.1 28.8 %copy-start.3 = (bf16[3584]{0:T(1024)(128)(2,1)S(1)}, bf16[3584]{0:T(1024)(128)(2,1)}, u32[]{:S(2)}) copy-start(bf16[3584]{0:T(1024)(128)(2,1)} %param.17) | copy-start | bytes 21508
  49.6 27.7 %copy-start.5 = (f32[2]{0:T(128)S(1)}, f32[2]{0:T(128)}, u32[]{:S(2)}) copy-start(f32[2]{0:T(128)} %param.15) | copy-start | bytes 28
  49.6 382.2 %copy-start.6 = (s32[128]{0:T(128)S(1)}, s32[128]{0:T(128)}, u32[]{:S(2)}) copy-start(s32[128]{0:T(128)} %param.16) | copy-start | bytes 1540
  447.3 3.7 copy-start.1
where the time goes:
time: 457 us
  blocking collectives  404 us (88%)
  local copies, waits for them, and re-layouts  22 us (5%)
  starting transfers between devices  15.6 us (3%)
  other arithmetic  12.1 us (3%)
    pmax x1, blocking collectives, local(): peak = lax.pmax(jnp.max(logits), 'dom')  214 us
    psum x1, blocking collectives, local(): total = lax.psum(jnp.sum(jnp.exp(logits - peak)), 'dom')  139 us
    all_gather x3, blocking collectives, merged(): gathered = jax.tree.map(lambda a: lax.all_gather(a, axis), part)  39 us
    ppermute x4, starting transfers between devices, shifted(): return lax.ppermute(value, axis, pairs)  15.6 us
    gather x4, local copies, waits for them, and re-layouts, local(): picked = jnp.take(arrived, slot, axis=0)  14.6 us
    all_gather x1, blocking collectives, local(): lax.all_gather(query, 'tp', axis=1, tiled=True)  12 us
  transfers between devices with their start and end apart: 4, of which 0 were waited for; matrix products, arithmetic and copies ran while one was open for 5% of the time, Pallas kernels for 0%

commit v1 on v0

v1 whole, which is shorter than its diff:
```python
import functools

import jax
import jax.numpy as jnp
from jax import lax
from jax.experimental import pallas as pl
from jax.experimental.pallas import tpu as pltpu
from jax.sharding import PartitionSpec as P

HQ = 28
KVH = 4
HD = 128
GROUP = HQ // KVH
FEATURES = HQ * HD
REACH = 2
P_DEV = 2
TP = 8
ROWS = 32
OWN = ROWS // TP
PAD_GROUP = ROWS // KVH
PART = ROWS + 8
TILE = 16

MASKED = -1e30
EPSILON = 1e-06

ANY = pl.BlockSpec(memory_space=pl.ANY)
SMEM = pl.BlockSpec(memory_space=pltpu.SMEM)
VMEM = pl.BlockSpec(memory_space=pltpu.VMEM)


def shifted(value, axis, by):
    devices = lax.axis_size(axis)
    pairs = [(i, i + by) for i in range(devices) if 0 <= i + by < devices]
    return lax.ppermute(value, axis, pairs)


def patch(block, first_row, row, fresh):
    inside = row - first_row
    tile = pl.multiple_of((inside // TILE) * TILE, TILE)
    old = block[pl.ds(tile, TILE), :].astype(jnp.float32)
    here = lax.broadcasted_iota(jnp.int32, old.shape, 0) == inside - tile
    block[pl.ds(tile, TILE), :] = jnp.where(here, fresh, old).astype(block.dtype)


def pick(ancestors, device, receivers):
    count = ancestors.shape[0]
    chosen = jnp.int32(0)
    for receiver in reversed(receivers):
        for slot in range(P_DEV):
            lane = P_DEV * receiver + slot
            wanted = ancestors[jnp.clip(lane, 0, count - 1)]
            fits = (lane >= 0) & (lane < count) & (wanted >> 1 == device)
            chosen = jnp.where(fits, wanted & 1, chosen)
    return chosen


def pack_kernel(far, ancestors, lengths, new_kv, cache, right, left, sems):
    device = lax.axis_index("dom")
    length = cache.shape[2]
    first = lax.axis_index("tp") * length
    copies = []
    for side, (out, sign) in enumerate(((right, 1), (left, -1))):
        receivers = [device + 2 * sign] if far else [device + sign, device + 2 * sign]
        particle = pick(ancestors, device, receivers)
        copy = pltpu.make_async_copy(cache.at[particle], out, sems.at[side])
        copy.start()
        copies.append((out, particle, copy))
    for out, particle, copy in copies:
        copy.wait()
        row = lengths[particle]

        @pl.when((row >= first) & (row < first + length))
        def _():
            fresh = new_kv[particle].astype(jnp.float32)
            for kv in range(2):
                patch(out.at[kv], first, row, fresh[kv : kv + 1])


def pack(ancestors, lengths, new_kv, cache, far):
    unit = jax.ShapeDtypeStruct(cache.shape[1:], cache.dtype)
    return pl.pallas_call(
        functools.partial(pack_kernel, far),
        out_shape=(unit, unit),
        in_specs=[SMEM, SMEM, VMEM, ANY],
        out_specs=(VMEM, VMEM),
        scratch_shapes=[pltpu.SemaphoreType.DMA((2,))],
        compiler_params=pltpu.CompilerParams(vmem_limit_bytes=16 << 20),
        name="pack_far" if far else "pack_near",
    )(ancestors, lengths, new_kv, cache)


def spread_query_kernel(query, out, wide):
    odd = lax.rem(lax.axis_index("tp"), 2)
    columns = query.shape[1]
    wide[...] = jnp.zeros_like(wide)
    wide[0:P_DEV, 0:columns] = query[...].astype(jnp.float32)
    even_rows = wide[...]
    odd_rows = pltpu.roll(even_rows, OWN * HD - columns, 1)
    rows = jnp.where(odd == 1, odd_rows, even_rows)
    for particle in range(P_DEV):
        for j in range(OWN):
            one = rows[particle : particle + 1, HD * j : HD * (j + 1)]
            for receiver in range(TP):
                out[receiver, pl.ds(OWN * particle + j, 1), :] = one


def spread_query(query):
    return pl.pallas_call(
        spread_query_kernel,
        out_shape=jax.ShapeDtypeStruct((TP, P_DEV * OWN, HD), jnp.float32),
        in_specs=[VMEM],
        out_specs=VMEM,
        scratch_shapes=[pltpu.VMEM((8, OWN * HD), jnp.float32)],
        name="spread_query",
    )(query)


def eye():
    shape = (ROWS, HD)
    return lax.broadcasted_iota(jnp.int32, shape, 0) == lax.broadcasted_iota(jnp.int32, shape, 1)


def attend_kernel(lengths, heads, new_kv, cache, out, kv, rows, sems):
    length = cache.shape[2]
    tp_index = lax.axis_index("tp")
    scale = HD ** (-0.5)
    copies = {}
    for particle in range(P_DEV):
        for half in range(2):
            copies[particle, half] = pltpu.make_async_copy(
                cache.at[particle, half], kv.at[particle, half], sems.at[particle, half]
            )
            copies[particle, half].start()
    row_index = lax.broadcasted_iota(jnp.int32, (ROWS, HD), 0)
    in_group = lax.rem(row_index, PAD_GROUP)
    wide_shape = (ROWS, KVH * HD)
    own_block = (
        lax.broadcasted_iota(jnp.int32, wide_shape, 0) // PAD_GROUP
        == lax.broadcasted_iota(jnp.int32, wide_shape, 1) // HD
    )
    for particle in range(P_DEV):
        for source in range(TP):
            rows[OWN * source : OWN * (source + 1), :] = heads[
                source, OWN * particle : OWN * (particle + 1), :
            ]
        parts = rows[...]
        after = pltpu.roll(parts, ROWS - 1, 0)
        before = pltpu.roll(parts, 1, 0)
        query = (
            parts
            + jnp.where(in_group == OWN - 1, after, 0.0)
            + jnp.where(in_group == OWN, before, 0.0)
        )
        fresh = new_kv[particle].astype(jnp.float32)
        own_key, own_value = [
            jnp.concatenate(
                [
                    jnp.broadcast_to(fresh[half : half + 1, HD * g : HD * (g + 1)], (PAD_GROUP, HD))
                    for g in range(KVH)
                ],
                axis=0,
            )
            for half in range(2)
        ]
        first_device = tp_index == 0
        own_score = jnp.sum(query * own_key, axis=1, keepdims=True) * scale
        own_score = jnp.where(first_device, own_score, MASKED)
        wide = jnp.concatenate([query] * KVH, axis=1)
        wide = jnp.where(own_block, wide, 0.0).astype(cache.dtype)
        copies[particle, 0].wait()
        scores = (
            lax.dot_general(
                wide, kv[particle, 0], (((1,), (1,)), ((), ())), preferred_element_type=jnp.float32
            )
            * scale
        )
        position = tp_index * length + lax.broadcasted_iota(jnp.int32, scores.shape, 1)
        valid = position < lengths[particle]
        scores = jnp.where(valid, scores, MASKED)
        block_max = jnp.max(scores, axis=1, keepdims=True)
        expo = jnp.where(valid, jnp.exp(scores - block_max), 0.0)
        block_sum = jnp.sum(expo, axis=1, keepdims=True)
        copies[particle, 1].wait()
        full = jnp.dot(
            expo.astype(cache.dtype), kv[particle, 1], preferred_element_type=jnp.float32
        )
        acc = jnp.concatenate(
            [
                full[PAD_GROUP * g : PAD_GROUP * (g + 1), HD * g : HD * (g + 1)]
                for g in range(KVH)
            ],
            axis=0,
        )
        top = jnp.maximum(block_max, own_score)
        factor = jnp.exp(block_max - top)
        own_factor = jnp.where(first_device, jnp.exp(own_score - top), 0.0)
        acc = factor * acc + own_factor * own_value
        total = factor * block_sum + own_factor
        diagonal = eye()
        top_row = jnp.sum(jnp.where(diagonal, top, 0.0), axis=0, keepdims=True)
        total_row = jnp.sum(jnp.where(diagonal, total, 0.0), axis=0, keepdims=True)
        stats_row = lax.broadcasted_iota(jnp.int32, (8, HD), 0)
        stats = jnp.where(stats_row == 0, top_row, jnp.where(stats_row == 1, total_row, 0.0))
        for receiver in range(TP):
            out[receiver, PART * particle : PART * particle + ROWS, :] = acc
            out[receiver, PART * particle + ROWS : PART * (particle + 1), :] = stats


def attend(lengths, heads, new_kv, cache):
    return pl.pallas_call(
        attend_kernel,
        out_shape=jax.ShapeDtypeStruct((TP, P_DEV * PART, HD), jnp.float32),
        in_specs=[SMEM, VMEM, VMEM, ANY],
        out_specs=VMEM,
        scratch_shapes=[
            pltpu.VMEM(cache.shape, cache.dtype),
            pltpu.VMEM((ROWS, HD), jnp.float32),
            pltpu.SemaphoreType.DMA((P_DEV, 2)),
        ],
        compiler_params=pltpu.CompilerParams(vmem_limit_bytes=16 << 20),
        name="attend",
    )(lengths, heads, new_kv, cache)


def merge_kernel(prior, parts, weight, attn, logits, weights, own_rows, wide):
    tp_index = lax.axis_index("tp")
    for g in range(KVH):
        for half in range(2):
            at = PAD_GROUP * g + OWN * half
            head = GROUP * g + (OWN - 1) * half
            weights[at : at + OWN, :] = weight[head : head + OWN, :]
    in_group = lax.rem(lax.broadcasted_iota(jnp.int32, (ROWS, HD), 0), PAD_GROUP)
    lane = lax.broadcasted_iota(jnp.int32, (ROWS, HD), 1)
    counted = ((in_group != OWN - 1) | (lane < HD // 2)) & ((in_group != OWN) | (lane >= HD // 2))
    diagonal = eye()
    logit_lane = lax.broadcasted_iota(jnp.int32, (1, HD), 1)
    logit_row = jnp.zeros((1, HD), jnp.float32)
    wide[...] = jnp.zeros_like(wide)
    for particle in range(P_DEV):
        at = PART * particle
        tops, totals = [
            [
                jnp.sum(
                    jnp.where(diagonal, parts[source, at + ROWS + k : at + ROWS + k + 1, :], 0.0),
                    axis=1,
                    keepdims=True,
                )
                for source in range(TP)
            ]
            for k in range(2)
        ]
        top = functools.reduce(jnp.maximum, tops)
        denom = jnp.zeros_like(top)
        numer = jnp.zeros((ROWS, HD), jnp.float32)
        for source in range(TP):
            factor = jnp.exp(tops[source] - top)
            denom = denom + factor * totals[source]
            numer = numer + factor * parts[source, at : at + ROWS, :]
        attended = numer / denom
        kept = jnp.where(counted, attended, 0.0)
        mean = jnp.sum(kept * kept) / FEATURES
        weighed = jnp.sum(weights[...] * kept)
        reward = jnp.full((1, HD), weighed) / jnp.sqrt(jnp.full((1, HD), mean) + EPSILON)
        logit_row = jnp.where(logit_lane == particle, prior[particle] + reward, logit_row)
        own_rows[...] = attended
        for j in range(OWN):
            wide[particle : particle + 1, HD * j : HD * (j + 1)] = own_rows[
                pl.ds(OWN * tp_index + j, 1), :
            ]
    columns = attn.shape[1]
    even = wide[...]
    odd = pltpu.roll(even, columns, 1)
    chosen = jnp.where(lax.rem(tp_index, 2) == 1, odd, even)
    attn[...] = chosen[0:P_DEV, 0:columns].astype(attn.dtype)
    logits[...] = jnp.broadcast_to(logit_row[None], logits.shape)


def merge(prior, parts, weight, columns, devices):
    return pl.pallas_call(
        merge_kernel,
        out_shape=(
            jax.ShapeDtypeStruct((P_DEV, columns), jnp.bfloat16),
            jax.ShapeDtypeStruct((devices, 1, HD), jnp.float32),
        ),
        in_specs=[SMEM, VMEM, VMEM],
        out_specs=(VMEM, VMEM),
        scratch_shapes=[
            pltpu.VMEM((ROWS, HD), jnp.float32),
            pltpu.VMEM((ROWS, HD), jnp.float32),
            pltpu.VMEM((8, OWN * HD), jnp.float32),
        ],
        name="merge",
    )(prior, parts, weight)


SPLIT = 2


def assemble_kernel(
    ancestors, lengths, logits, new_kv, cache, right1, left1, right2, left2,
    new_cache, log_weight, buffer, in_sems, out_sems,
):
    device = lax.axis_index("dom")
    length = cache.shape[2]
    first = lax.axis_index("tp") * length
    rows = length // SPLIT
    pieces = [
        (slot, kv, part) for part in range(SPLIT) for kv in range(2) for slot in range(P_DEV)
    ]
    owner = [ancestors[P_DEV * device + slot] for slot in range(P_DEV)]

    def arriving(ref, piece):
        slot, kv, part = piece
        at = pl.ds(part * rows, rows)
        return pltpu.make_async_copy(ref.at[kv, at], buffer.at[slot, kv, at], in_sems.at[slot, kv, part])

    for piece in pieces:
        offset = (owner[piece[0]] >> 1) - device

        @pl.when(offset == 0)
        def _():
            arriving(cache.at[owner[piece[0]] & 1], piece).start()

        for at, ref in ((-1, right1), (1, left1), (-2, right2), (2, left2)):

            @pl.when(offset == at)
            def _():
                arriving(ref, piece).start()

    lane = lax.broadcasted_iota(jnp.int32, (logits.shape[0], HD), 1)
    every = jnp.where(lane < P_DEV, logits[:, 0, :], -jnp.inf)
    peak = jnp.max(jnp.max(every, axis=1, keepdims=True), axis=0, keepdims=True)
    terms = jnp.exp(every - peak)
    total = jnp.sum(jnp.sum(terms, axis=1, keepdims=True), axis=0, keepdims=True)
    mine = logits[device] - (peak + jnp.log(total))
    for slot in range(P_DEV):
        log_weight[slot] = mine[0, slot]

    leaving = []
    for piece in pieces:
        slot, kv, part = piece
        at = pl.ds(part * rows, rows)
        arriving(right1, piece).wait()
        particle = owner[slot] & 1
        row = lengths[particle] - (first + part * rows)

        @pl.when((owner[slot] >> 1 == device) & (row >= 0) & (row < rows))
        def _():
            fresh = new_kv[particle].astype(jnp.float32)
            patch(buffer.at[slot, kv], 0, row + part * rows, fresh[kv : kv + 1])

        copy = pltpu.make_async_copy(
            buffer.at[slot, kv, at], new_cache.at[slot, kv, at], out_sems.at[slot, kv, part]
        )
        copy.start()
        leaving.append(copy)
    for copy in leaving:
        copy.wait()


def assemble(ancestors, lengths, logits, new_kv, cache, right1, left1, right2, left2):
    return pl.pallas_call(
        assemble_kernel,
        out_shape=(
            jax.ShapeDtypeStruct(cache.shape, cache.dtype),
            jax.ShapeDtypeStruct((P_DEV,), jnp.float32),
        ),
        in_specs=[SMEM, SMEM, VMEM, VMEM, ANY, ANY, ANY, ANY, ANY],
        out_specs=(ANY, SMEM),
        scratch_shapes=[
            pltpu.VMEM(cache.shape, cache.dtype),
            pltpu.SemaphoreType.DMA((P_DEV, 2, SPLIT)),
            pltpu.SemaphoreType.DMA((P_DEV, 2, SPLIT)),
        ],
        compiler_params=pltpu.CompilerParams(vmem_limit_bytes=16 << 20),
        name="assemble",
    )(ancestors, lengths, logits, new_kv, cache, right1, left1, right2, left2)


def crowded(ancestors):
    source = ancestors // P_DEV
    offset = source - jnp.arange(ancestors.shape[0], dtype=jnp.int32) // P_DEV
    found = jnp.bool_(False)
    for ahead in range(1, 2 * P_DEV):
        here, there = slice(None, -ahead), slice(ahead, None)
        both = (source[here] == source[there]) & (ancestors[here] != ancestors[there])
        right = (offset[here] == -1) & (offset[there] == -2)
        left = (offset[here] == 2) & (offset[there] == 1)
        found = found | jnp.any(both & (right | left))
    return found


def local(query, new_kv, cache, lengths, prior_logw, ancestors, w_reward):
    right0, left0 = pack(ancestors, lengths, new_kv, cache, far=False)
    right1 = shifted(right0, "dom", 1)
    left1 = shifted(left0, "dom", -1)
    heads = lax.all_to_all(spread_query(query), "tp", 0, 0)
    parts = attend(lengths, heads, new_kv, cache)
    parts = lax.all_to_all(parts, "tp", 0, 0)
    parts, right1, left1 = lax.optimization_barrier((parts, right1, left1))
    right2 = shifted(right1, "dom", 1)
    left2 = shifted(left1, "dom", -1)
    weight = w_reward.astype(jnp.float32).reshape(HQ, HD)
    attn, logits = merge(prior_logw, parts, weight, query.shape[1], lax.axis_size("dom"))
    logits = lax.all_to_all(logits, "dom", 0, 0)

    def near(right2, left2):
        return assemble(ancestors, lengths, logits, new_kv, cache, right1, left1, right2, left2)

    def direct(right2, left2):
        right0, left0 = pack(ancestors, lengths, new_kv, cache, far=True)
        return near(shifted(right0, "dom", REACH), shifted(left0, "dom", -REACH))

    new_cache, log_weight = lax.cond(crowded(ancestors), direct, near, right2, left2)
    return (attn, log_weight, new_cache)


def solution(mesh):
    in_specs = (
        P("dom", "tp"),
        P("dom", None, None),
        P("dom", None, "tp", None),
        P("dom"),
        P("dom"),
        P(),
        P(),
    )
    out_specs = (P("dom", "tp"), P("dom"), P("dom", None, "tp", None))
    return jax.shard_map(local, mesh=mesh, in_specs=in_specs, out_specs=out_specs, check_vma=False)
```

time: 457 us -> 83.6 us (0.18)
  the two profiles are of different devices: /device:TPU:6 before, /device:TPU:8 now
where the time goes in v1:
time: 83.6 us; the launch traced here: 83 us
  starting transfers between devices  30.6 us (37%)
  blocking collectives  21.1 us (25%)
  waiting for transfers between devices  13.2 us (16%)
  Pallas kernels  12.6 us (15%)
  other arithmetic  2.73 us (3%)
  between operations  2.7 us (3%)
    ppermute x4, starting transfers between devices, shifted(): return lax.ppermute(value, axis, pairs)  20.7 us
    all_to_all x1, waiting for transfers between devices, local(): logits = lax.all_to_all(logits, 'dom', 0, 0)  13.2 us
    all_to_all x1, blocking collectives, local(): parts = lax.all_to_all(parts, 'tp', 0, 0)  11.3 us
    all_to_all x1, starting transfers between devices, local(): logits = lax.all_to_all(logits, 'dom', 0, 0)  9.94 us
    all_to_all x1, blocking collectives, local(): heads = lax.all_to_all(spread_query(query), 'tp', 0, 0)  9.76 us
    pallas_call x1, Pallas kernels, assemble(): pl.pallas_call(assemble_kernel, out_shape=(jax.ShapeDtypeStruct(cache.sha...  3.92 us
    pallas_call x1, Pallas kernels, attend(): pl.pallas_call(attend_kernel, out_shape=jax.ShapeDtypeStruct((TP, P_DEV *...  2.9 us
    pallas_call x1, Pallas kernels, pack(): pl.pallas_call(functools.partial(pack_kernel, far), out_shape=(unit, unit...  2.43 us
  transfers between devices with their start and end apart: 5, of which 1 were waited for; matrix products, arithmetic and copies ran while one was open for 3% of the time, Pallas kernels for 8%

profile of v1, /device:TPU:8, one launch (start us, length us, event | category | flops | bytes accessed | tf_op | source)
XLA Modules:
  0.0 83.0 jit_solution(7319399010769190571)
XLA Ops:
  0.6 0.0 copy-start.3
  0.6 0.0 copy-start.1
  0.7 2.4 %pack_near.1 = (bf16[2,512,512]{2,1,0:T(8,128)(2,1)S(1)}, bf16[2,512,512]{2,1,0:T(8,128)(2,1)S(1)}) custom-call(s32[128]{0:T(128)} %ancestors.1, s32[2]{0:T(128)} %lengths.3, bf16[2,2,512]{2,1,0:T(2,128)(2,1)} %new_kv.3, bf16[2,2,512,512]{3,2,1,0:T(8,128)(2,1)} %cache.3), custom_call_target="tpu_custom_call" | custom-call | tf_op jit(solution)/shard_map/pack_near/pallas_call | solution.py:82
  3.1 0.0 copy-start.2
  3.1 0.0 copy-start.4
  3.1 4.2 %collective-permute-start.2 = (bf16[2,512,512]{2,1,0:T(8,128)(2,1)S(1)}, bf16[2,512,512]{2,1,0:T(8,128)(2,1)S(1)}, u32[]{:S(2)}, u32[]{:S(2)}) collective-permute-start(bf16[2,512,512]{2,1,0:T(8,128)(2,1)S(1)} %get-tuple-element.62), channel_id=1, source_target_pairs={{0,8},{8,16},{16,24},{24,32},{32,40},{40,48},{48,56},{56,64},{64,7... | collective-permute-start | bytes 3145736 | tf_op jit(solution)/shard_map/ppermute | solution.py:35
  7.4 8.5 %collective-permute-start.3 = (bf16[2,512,512]{2,1,0:T(8,128)(2,1)S(1)}, bf16[2,512,512]{2,1,0:T(8,128)(2,1)}, u32[]{:S(2)}, u32[]{:S(2)}) collective-permute-start(bf16[2,512,512]{2,1,0:T(8,128)(2,1)S(1)} %get-tuple-element.63), channel_id=1, source_target_pairs={{8,0},{16,8},{24,16},{32,24},{40,32},{48,40},{56,48},{64,56},{72,6... | collective-permute-start | bytes 3145736 | tf_op jit(solution)/shard_map/ppermute | solution.py:35
  15.9 1.4 %spread_query.1 = f32[8,8,128]{2,1,0:T(8,128)} custom-call(bf16[2,448]{1,0:T(2,128)(2,1)} %query.1), custom_call_target="tpu_custom_call" | custom-call | tf_op jit(solution)/shard_map/spread_query/pallas_call | solution.py:109
  17.3 9.8 %all_to_all.15.heads = f32[8,8,128]{2,1,0:T(8,128)S(1)} all-to-all(f32[8,8,128]{2,1,0:T(8,128)} %spread_query.1), channel_id=1, replica_groups=mesh['dom'=64,'tp'=8] {'tp'}, dimensions={0} | all-to-all | bytes 65536 | tf_op jit(solution)/shard_map/all_to_all | solution.py:398
  27.0 0.0 copy-done.3
  27.0 0.0 copy-done.1
  27.0 2.9 %attend.1 = f32[8,80,128]{2,1,0:T(8,128)S(1)} custom-call(s32[2]{0:T(128)S(1)} %copy-done.3, f32[8,8,128]{2,1,0:T(8,128)S(1)} %all_to_all.15.heads, bf16[2,2,512]{2,1,0:T(2,128)(2,1)S(1)} %copy-done.1, bf16[2,2,512,512]{3,2,1,0:T(8,128)(2,1)} %cache.3), custom_call_target="tpu_custom_call" | custom-call | tf_op jit(solution)/shard_map/attend/pallas_call | solution.py:211
  30.0 11.3 %all_to_all.16.parts = f32[8,80,128]{2,1,0:T(8,128)} all-to-all(f32[8,80,128]{2,1,0:T(8,128)S(1)} %attend.1), channel_id=1, replica_groups=mesh['dom'=64,'tp'=8] {'tp'}, dimensions={0} | all-to-all | bytes 655360 | tf_op jit(solution)/shard_map/all_to_all | solution.py:400
  41.3 0.0 collective-permute-done.2
  41.3 0.0 collective-permute-done.3
  41.3 1.9 %collective-permute-start.4 = (bf16[2,512,512]{2,1,0:T(8,128)(2,1)S(1)}, bf16[2,512,512]{2,1,0:T(8,128)(2,1)S(1)}, u32[]{:S(2)}, u32[]{:S(2)}) collective-permute-start(bf16[2,512,512]{2,1,0:T(8,128)(2,1)S(1)} %collective-permute-done.2), channel_id=1, source_target_pairs={{0,8},{8,16},{16,24},{24,32},{32,40},{40,48},{48,56},{56,64},{64,7... | collective-permute-start | bytes 3145736 | tf_op jit(solution)/shard_map/ppermute | solution.py:35
  43.2 6.0 %collective-permute-start.5 = (bf16[2,512,512]{2,1,0:T(8,128)(2,1)}, bf16[2,512,512]{2,1,0:T(8,128)(2,1)S(1)}, u32[]{:S(2)}, u32[]{:S(2)}) collective-permute-start(bf16[2,512,512]{2,1,0:T(8,128)(2,1)} %collective-permute-done.3), channel_id=1, source_target_pairs={{8,0},{16,8},{24,16},{32,24},{40,32},{48,40},{56,48},{64,56},{72,6... | collective-permute-start | bytes 3145736 | tf_op jit(solution)/shard_map/ppermute | solution.py:35
  49.2 0.0 copy-done.2
  49.3 0.7 and_reduce_fusion.2
  50.0 0.7 and_reduce_fusion.1
  52.0 0.0 copy-done.4
  52.0 0.6 bitcast_convert_fusion.weight
  52.6 2.0 %merge.1 = (bf16[2,448]{1,0:T(2,128)(2,1)}, f32[64,1,128]{2,1,0:T(1,128)}) custom-call(f32[2]{0:T(128)} %prior.1, f32[8,80,128]{2,1,0:T(8,128)} %all_to_all.16.parts, f32[28,128]{1,0:T(8,128)} %bitcast_convert_fusion.weight), custom_call_target="tpu_custom_call" | custom-call | tf_op jit(solution)/shard_map/merge/pallas_call | solution.py:280
  54.6 9.9 %all-to-all-start.2 = ((f32[64,1,128]{2,1,0:T(1,128)}), f32[64,1,128]{2,1,0:T(1,128)S(1)}, u32[]{:S(2)}, u32[]{:S(2)}) async-start(f32[64,1,128]{2,1,0:T(1,128)} %get-tuple-element.66), calls=%async_computation.2 | async-start | bytes 65536 | tf_op jit(solution)/shard_map/all_to_all | solution.py:406
  64.5 0.7 and_reduce_fusion
  65.9 13.2 %all-to-all-done.2 = f32[64,1,128]{2,1,0:T(1,128)S(1)} async-done(((f32[64,1,128]{2,1,0:T(1,128)}), f32[64,1,128]{2,1,0:T(1,128)S(1)}, u32[]{:S(2)}, u32[]{:S(2)}) %all-to-all-start.2) | async-done | bytes 32800 | tf_op jit(solution)/shard_map/all_to_all | solution.py:406
  79.1 0.0 collective-permute-done.4
  79.1 0.0 collective-permute-done.5
  79.1 3.9 %conditional.1 = ((bf16[2,2,512,512]{3,2,1,0:T(8,128)(2,1)}, f32[2]{0:T(128)})) conditional(s32[]{:T(128)} %convert_element_type.4, (s32[128]{0:T(128)S(1)}, s32[2]{0:T(128)S(1)}, f32[64,1,128]{2,1,0:T(1,128)S(1)}, bf16[2,2,512]{2,1,0:T(2,128)(2,1)S(1)}, bf16[2,2,512,512]{3,2,1,0:T(8,128)(2,1)}, /*index=5*/bf16[2,512,512]{2,1,0:T(8,128)(2,1)S(1)}, ...), branch_computations={%region_3.4_spmd, %region_4.5_spmd} | conditional | bytes 16777332 | solution.py:415
  79.1 3.9 %assemble.2 = (bf16[2,2,512,512]{3,2,1,0:T(8,128)(2,1)}, f32[2]{0:T(128)}) custom-call(s32[128]{0:T(128)S(1)} %get-tuple-element.32.ancestors, s32[2]{0:T(128)S(1)} %get-tuple-element.33.lengths, f32[64,1,128]{2,1,0:T(1,128)S(1)} %get-tuple-element.34.logits, bf16[2,2,512]{2,1,0:T(2,128)(2,1)S(1)} %get-tuple-element.35.new_kv, ...), custom_call_target="tpu_custom_call" | custom-call | tf_op jit(solution)/shard_map/cond/branch_0_fun/assemble/pallas_call | solution.py:363
  (1 shorter events, 0.0 us)
Async XLA Ops:
  0.6 26.4 %copy-start.3 = (s32[2]{0:T(128)S(1)}, s32[2]{0:T(128)}, u32[]{:S(2)}) copy-start(s32[2]{0:T(128)} %lengths.3) | copy-start | bytes 28
  0.6 26.4 %copy-start.1 = (bf16[2,2,512]{2,1,0:T(2,128)(2,1)S(1)}, bf16[2,2,512]{2,1,0:T(2,128)(2,1)}, u32[]{:S(2)}) copy-start(bf16[2,2,512]{2,1,0:T(2,128)(2,1)} %new_kv.3) | copy-start | bytes 12292
  3.1 46.1 %copy-start.2 = (s32[128]{0:T(128)S(1)}, s32[128]{0:T(128)}, u32[]{:S(2)}) copy-start(s32[128]{0:T(128)} %ancestors.1) | copy-start | bytes 1540
  3.1 48.9 %copy-start.4 = (bf16[3584]{0:T(1024)(128)(2,1)S(1)}, bf16[3584]{0:T(1024)(128)(2,1)}, u32[]{:S(2)}) copy-start(bf16[3584]{0:T(1024)(128)(2,1)} %param.15) | copy-start | bytes 21508
  3.1 38.2 %collective-permute-start.2 = (bf16[2,512,512]{2,1,0:T(8,128)(2,1)S(1)}, bf16[2,512,512]{2,1,0:T(8,128)(2,1)S(1)}, u32[]{:S(2)}, u32[]{:S(2)}) collective-permute-start(bf16[2,512,512]{2,1,0:T(8,128)(2,1)S(1)} %get-tuple-element.62), channel_id=1, source_target_pairs={{0,8},{8,16},{16,24},{24,32},{32,40},{40,48},{48,56},{56,64},{64,7... | collective-permute-start | bytes 3145736 | tf_op jit(solution)/shard_map/ppermute | solution.py:35
  7.4 33.9 %collective-permute-start.3 = (bf16[2,512,512]{2,1,0:T(8,128)(2,1)S(1)}, bf16[2,512,512]{2,1,0:T(8,128)(2,1)}, u32[]{:S(2)}, u32[]{:S(2)}) collective-permute-start(bf16[2,512,512]{2,1,0:T(8,128)(2,1)S(1)} %get-tuple-element.63), channel_id=1, source_target_pairs={{8,0},{16,8},{24,16},{32,24},{40,32},{48,40},{56,48},{64,56},{72,6... | collective-permute-start | bytes 3145736 | tf_op jit(solution)/shard_map/ppermute | solution.py:35
  41.3 37.8 %collective-permute-start.4 = (bf16[2,512,512]{2,1,0:T(8,128)(2,1)S(1)}, bf16[2,512,512]{2,1,0:T(8,128)(2,1)S(1)}, u32[]{:S(2)}, u32[]{:S(2)}) collective-permute-start(bf16[2,512,512]{2,1,0:T(8,128)(2,1)S(1)} %collective-permute-done.2), channel_id=1, source_target_pairs={{0,8},{8,16},{16,24},{24,32},{32,40},{40,48},{48,56},{56,64},{64,7... | collective-permute-start | bytes 3145736 | tf_op jit(solution)/shard_map/ppermute | solution.py:35
  43.2 35.9 %collective-permute-start.5 = (bf16[2,512,512]{2,1,0:T(8,128)(2,1)}, bf16[2,512,512]{2,1,0:T(8,128)(2,1)S(1)}, u32[]{:S(2)}, u32[]{:S(2)}) collective-permute-start(bf16[2,512,512]{2,1,0:T(8,128)(2,1)} %collective-permute-done.3), channel_id=1, source_target_pairs={{8,0},{16,8},{24,16},{32,24},{40,32},{48,40},{56,48},{64,56},{72,6... | collective-permute-start | bytes 3145736 | tf_op jit(solution)/shard_map/ppermute | solution.py:35
  54.6 24.5 %all-to-all-start.2 = ((f32[64,1,128]{2,1,0:T(1,128)}), f32[64,1,128]{2,1,0:T(1,128)S(1)}, u32[]{:S(2)}, u32[]{:S(2)}) async-start(f32[64,1,128]{2,1,0:T(1,128)} %get-tuple-element.66), calls=%async_computation.2 | async-start | bytes 65536 | tf_op jit(solution)/shard_map/all_to_all | solution.py:406

commit v2 on v1

--- a/solution.py
+++ b/solution.py
@@ -25,6 +25,7 @@
 EPSILON = 1e-06
 
 ANY = pl.BlockSpec(memory_space=pl.ANY)
+HBM = pl.BlockSpec(memory_space=pltpu.HBM)
 SMEM = pl.BlockSpec(memory_space=pltpu.SMEM)
 VMEM = pl.BlockSpec(memory_space=pltpu.VMEM)
 
@@ -32,6 +33,13 @@
 def shifted(value, axis, by):
     devices = lax.axis_size(axis)
     pairs = [(i, i + by) for i in range(devices) if 0 <= i + by < devices]
+    return lax.ppermute(value, axis, pairs)
+
+
+def swapped(value, axis, first):
+    pairs = []
+    for i in range(first, lax.axis_size(axis) - 1, 2):
+        pairs += [(i, i + 1), (i + 1, i)]
     return lax.ppermute(value, axis, pairs)
 
 
@@ -55,65 +63,126 @@
     return chosen
 
 
-def pack_kernel(far, ancestors, lengths, new_kv, cache, right, left, sems):
+def crowded(ancestors):
+    count = ancestors.shape[1]
+    shape = (8, count)
+    wanted = jnp.broadcast_to(ancestors[...], shape)
+    lane = lax.broadcasted_iota(jnp.int32, shape, 1)
+    offset = (wanted >> 1) - (lane >> 1)
+    found = jnp.zeros(shape, jnp.float32)
+    for ahead in range(1, 2 * P_DEV):
+        later_wanted = pltpu.roll(wanted, count - ahead, 1)
+        later_offset = pltpu.roll(offset, count - ahead, 1)
+        differ = (wanted >> 1 == later_wanted >> 1) & (wanted != later_wanted)
+        sides = ((offset == -1) & (later_offset == -2)) | ((offset == 2) & (later_offset == 1))
+        found = jnp.where(differ & sides & (lane < count - ahead), 1.0, found)
+    return (jnp.sum(found) > 0.0).astype(jnp.int32)
+
+
+def pad_query(query, out, wide):
+    columns = query.shape[1]
+    wide[...] = jnp.zeros_like(wide)
+    wide[0:P_DEV, 0:columns] = query[...].astype(jnp.float32)
+    even_rows = wide[...]
+    odd_rows = pltpu.roll(even_rows, OWN * HD - columns, 1)
+    rows = jnp.where(lax.rem(lax.axis_index("tp"), 2) == 1, odd_rows, even_rows)
+    for particle in range(P_DEV):
+        for j in range(OWN):
+            one = rows[particle : particle + 1, HD * j : HD * (j + 1)]
+            for receiver in range(TP):
+                out[receiver, pl.ds(OWN * particle + j, 1), :] = one
+
+
+def pack_kernel(
+    ancestors, lengths, row, query, new_kv, cache, even, odd, rows, flag, asked, fresh, wide, sems, small_sems
+):
+    device = lax.axis_index("dom")
+    length = cache.shape[2]
+    first = lax.axis_index("tp") * length
+    small = [
+        pltpu.make_async_copy(query, asked, small_sems.at[0]),
+        pltpu.make_async_copy(new_kv, fresh, small_sems.at[1]),
+    ]
+    facing = 1 - 2 * (device & 1)
+    units = []
+    for side, (out, sign) in enumerate(((even, facing), (odd, -facing))):
+        particle = pick(ancestors, device, [device + sign, device + 2 * sign])
+        for kv in range(2):
+            copy = pltpu.make_async_copy(cache.at[particle, kv], out.at[kv], sems.at[side, kv])
+            copy.start()
+            units.append((out, particle, kv, copy))
+    for copy in small:
+        copy.start()
+    flag[0] = crowded(row)
+    for copy in small:
+        copy.wait()
+    pad_query(asked, rows, wide)
+    for out, particle, kv, copy in units:
+        copy.wait()
+        position = lengths[particle]
+
+        @pl.when((position >= first) & (position < first + length))
+        def _():
+            new = fresh[particle].astype(jnp.float32)
+            patch(out.at[kv], first, position, new[kv : kv + 1])
+
+
+def pack(ancestors, lengths, query, new_kv, cache):
+    unit = jax.ShapeDtypeStruct(cache.shape[1:], cache.dtype)
+    return pl.pallas_call(
+        pack_kernel,
+        out_shape=(
+            unit,
+            unit,
+            jax.ShapeDtypeStruct((TP, P_DEV * OWN, HD), jnp.float32),
+            jax.ShapeDtypeStruct((1,), jnp.int32),
+        ),
+        in_specs=[SMEM, SMEM, VMEM, HBM, HBM, HBM],
+        out_specs=(VMEM, VMEM, VMEM, SMEM),
+        scratch_shapes=[
+            pltpu.VMEM(query.shape, query.dtype),
+            pltpu.VMEM(new_kv.shape, new_kv.dtype),
+            pltpu.VMEM((8, OWN * HD), jnp.float32),
+            pltpu.SemaphoreType.DMA((P_DEV, 2)),
+            pltpu.SemaphoreType.DMA((2,)),
+        ],
+        compiler_params=pltpu.CompilerParams(vmem_limit_bytes=16 << 20),
+        name="pack",
+    )(ancestors, lengths, ancestors.reshape(1, -1), query, new_kv, cache)
+
+
+def pack_far_kernel(ancestors, lengths, new_kv, cache, right, left, sems):
     device = lax.axis_index("dom")
     length = cache.shape[2]
     first = lax.axis_index("tp") * length
     copies = []
     for side, (out, sign) in enumerate(((right, 1), (left, -1))):
-        receivers = [device + 2 * sign] if far else [device + sign, device + 2 * sign]
-        particle = pick(ancestors, device, receivers)
+        particle = pick(ancestors, device, [device + REACH * sign])
         copy = pltpu.make_async_copy(cache.at[particle], out, sems.at[side])
         copy.start()
         copies.append((out, particle, copy))
     for out, particle, copy in copies:
         copy.wait()
-        row = lengths[particle]
-
-        @pl.when((row >= first) & (row < first + length))
+        position = lengths[particle]
+
+        @pl.when((position >= first) & (position < first + length))
         def _():
             fresh = new_kv[particle].astype(jnp.float32)
             for kv in range(2):
-                patch(out.at[kv], first, row, fresh[kv : kv + 1])
-
-
-def pack(ancestors, lengths, new_kv, cache, far):
+                patch(out.at[kv], first, position, fresh[kv : kv + 1])
+
+
+def pack_far(ancestors, lengths, new_kv, cache):
     unit = jax.ShapeDtypeStruct(cache.shape[1:], cache.dtype)
     return pl.pallas_call(
-        functools.partial(pack_kernel, far),
+        pack_far_kernel,
         out_shape=(unit, unit),
         in_specs=[SMEM, SMEM, VMEM, ANY],
         out_specs=(VMEM, VMEM),
-        scratch_shapes=[pltpu.SemaphoreType.DMA((2,))],
+        scratch_shapes=[pltpu.SemaphoreType.DMA((P_DEV,))],
         compiler_params=pltpu.CompilerParams(vmem_limit_bytes=16 << 20),
-        name="pack_far" if far else "pack_near",
+        name="pack_far",
     )(ancestors, lengths, new_kv, cache)
-
-
-def spread_query_kernel(query, out, wide):
-    odd = lax.rem(lax.axis_index("tp"), 2)
-    columns = query.shape[1]
-    wide[...] = jnp.zeros_like(wide)
-    wide[0:P_DEV, 0:columns] = query[...].astype(jnp.float32)
-    even_rows = wide[...]
-    odd_rows = pltpu.roll(even_rows, OWN * HD - columns, 1)
-    rows = jnp.where(odd == 1, odd_rows, even_rows)
-    for particle in range(P_DEV):
-        for j in range(OWN):
-            one = rows[particle : particle + 1, HD * j : HD * (j + 1)]
-            for receiver in range(TP):
-                out[receiver, pl.ds(OWN * particle + j, 1), :] = one
-
-
-def spread_query(query):
-    return pl.pallas_call(
-        spread_query_kernel,
-        out_shape=jax.ShapeDtypeStruct((TP, P_DEV * OWN, HD), jnp.float32),
-        in_specs=[VMEM],
-        out_specs=VMEM,
-        scratch_shapes=[pltpu.VMEM((8, OWN * HD), jnp.float32)],
-        name="spread_query",
-    )(query)
 
 
 def eye():
@@ -121,17 +190,10 @@
     return lax.broadcasted_iota(jnp.int32, shape, 0) == lax.broadcasted_iota(jnp.int32, shape, 1)
 
 
-def attend_kernel(lengths, heads, new_kv, cache, out, kv, rows, sems):
-    length = cache.shape[2]
+def attend_kernel(lengths, heads, new_kv, kv, out, rows):
+    length = kv.shape[2]
     tp_index = lax.axis_index("tp")
     scale = HD ** (-0.5)
-    copies = {}
-    for particle in range(P_DEV):
-        for half in range(2):
-            copies[particle, half] = pltpu.make_async_copy(
-                cache.at[particle, half], kv.at[particle, half], sems.at[particle, half]
-            )
-            copies[particle, half].start()
     row_index = lax.broadcasted_iota(jnp.int32, (ROWS, HD), 0)
     in_group = lax.rem(row_index, PAD_GROUP)
     wide_shape = (ROWS, KVH * HD)
@@ -167,8 +229,7 @@
         own_score = jnp.sum(query * own_key, axis=1, keepdims=True) * scale
         own_score = jnp.where(first_device, own_score, MASKED)
         wide = jnp.concatenate([query] * KVH, axis=1)
-        wide = jnp.where(own_block, wide, 0.0).astype(cache.dtype)
-        copies[particle, 0].wait()
+        wide = jnp.where(own_block, wide, 0.0).astype(kv.dtype)
         scores = (
             lax.dot_general(
                 wide, kv[particle, 0], (((1,), (1,)), ((), ())), preferred_element_type=jnp.float32
@@ -181,9 +242,8 @@
         block_max = jnp.max(scores, axis=1, keepdims=True)
         expo = jnp.where(valid, jnp.exp(scores - block_max), 0.0)
         block_sum = jnp.sum(expo, axis=1, keepdims=True)
-        copies[particle, 1].wait()
         full = jnp.dot(
-            expo.astype(cache.dtype), kv[particle, 1], preferred_element_type=jnp.float32
+            expo.astype(kv.dtype), kv[particle, 1], preferred_element_type=jnp.float32
         )
         acc = jnp.concatenate(
             [
@@ -207,23 +267,19 @@
             out[receiver, PART * particle + ROWS : PART * (particle + 1), :] = stats
 
 
-def attend(lengths, heads, new_kv, cache):
+def attend(lengths, heads, new_kv, kept):
     return pl.pallas_call(
         attend_kernel,
         out_shape=jax.ShapeDtypeStruct((TP, P_DEV * PART, HD), jnp.float32),
-        in_specs=[SMEM, VMEM, VMEM, ANY],
+        in_specs=[SMEM, VMEM, VMEM, VMEM],
         out_specs=VMEM,
-        scratch_shapes=[
-            pltpu.VMEM(cache.shape, cache.dtype),
-            pltpu.VMEM((ROWS, HD), jnp.float32),
-            pltpu.SemaphoreType.DMA((P_DEV, 2)),
-        ],
+        scratch_shapes=[pltpu.VMEM((ROWS, HD), jnp.float32)],
         compiler_params=pltpu.CompilerParams(vmem_limit_bytes=16 << 20),
         name="attend",
-    )(lengths, heads, new_kv, cache)
-
-
-def merge_kernel(prior, parts, weight, attn, logits, weights, own_rows, wide):
+    )(lengths, heads, new_kv, kept)
+
+
+def merge_kernel(prior, parts, weight, attn, logits, weights, all_rows, wide):
     tp_index = lax.axis_index("tp")
     for g in range(KVH):
         for half in range(2):
@@ -263,9 +319,9 @@
         weighed = jnp.sum(weights[...] * kept)
         reward = jnp.full((1, HD), weighed) / jnp.sqrt(jnp.full((1, HD), mean) + EPSILON)
         logit_row = jnp.where(logit_lane == particle, prior[particle] + reward, logit_row)
-        own_rows[...] = attended
+        all_rows[...] = attended
         for j in range(OWN):
-            wide[particle : particle + 1, HD * j : HD * (j + 1)] = own_rows[
+            wide[particle : particle + 1, HD * j : HD * (j + 1)] = all_rows[
                 pl.ds(OWN * tp_index + j, 1), :
             ]
     columns = attn.shape[1]
@@ -290,6 +346,7 @@
             pltpu.VMEM((ROWS, HD), jnp.float32),
             pltpu.VMEM((8, OWN * HD), jnp.float32),
         ],
+        compiler_params=pltpu.CompilerParams(vmem_limit_bytes=8 << 20),
         name="merge",
     )(prior, parts, weight)
 
@@ -298,8 +355,7 @@
 
 
 def assemble_kernel(
-    ancestors, lengths, logits, new_kv, cache, right1, left1, right2, left2,
-    new_cache, log_weight, buffer, in_sems, out_sems,
+    far, ancestors, lengths, new_kv, cache, even1, odd1, even2, odd2, new_cache, buffer, in_sems, out_sems
 ):
     device = lax.axis_index("dom")
     length = cache.shape[2]
@@ -317,31 +373,29 @@
 
     for piece in pieces:
         offset = (owner[piece[0]] >> 1) - device
+        facing = offset * (1 - 2 * (device & 1))
+        two = offset if far else facing
 
         @pl.when(offset == 0)
         def _():
             arriving(cache.at[owner[piece[0]] & 1], piece).start()
 
-        for at, ref in ((-1, right1), (1, left1), (-2, right2), (2, left2)):
-
-            @pl.when(offset == at)
+        for found, ref in (
+            (facing == 1, even1),
+            (facing == -1, odd1),
+            (two == REACH, even2),
+            (two == -REACH, odd2),
+        ):
+
+            @pl.when(found)
             def _():
                 arriving(ref, piece).start()
-
-    lane = lax.broadcasted_iota(jnp.int32, (logits.shape[0], HD), 1)
-    every = jnp.where(lane < P_DEV, logits[:, 0, :], -jnp.inf)
-    peak = jnp.max(jnp.max(every, axis=1, keepdims=True), axis=0, keepdims=True)
-    terms = jnp.exp(every - peak)
-    total = jnp.sum(jnp.sum(terms, axis=1, keepdims=True), axis=0, keepdims=True)
-    mine = logits[device] - (peak + jnp.log(total))
-    for slot in range(P_DEV):
-        log_weight[slot] = mine[0, slot]
 
     leaving = []
     for piece in pieces:
         slot, kv, part = piece
         at = pl.ds(part * rows, rows)
-        arriving(right1, piece).wait()
+        arriving(even1, piece).wait()
         particle = owner[slot] & 1
         row = lengths[particle] - (first + part * rows)
 
@@ -359,15 +413,12 @@
         copy.wait()
 
 
-def assemble(ancestors, lengths, logits, new_kv, cache, right1, left1, right2, left2):
-    return pl.pallas_call(
-        assemble_kernel,
-        out_shape=(
-            jax.ShapeDtypeStruct(cache.shape, cache.dtype),
-            jax.ShapeDtypeStruct((P_DEV,), jnp.float32),
-        ),
-        in_specs=[SMEM, SMEM, VMEM, VMEM, ANY, ANY, ANY, ANY, ANY],
-        out_specs=(ANY, SMEM),
+def assemble(ancestors, lengths, new_kv, cache, even1, odd1, even2, odd2, far):
+    return pl.pallas_call(
+        functools.partial(assemble_kernel, far),
+        out_shape=jax.ShapeDtypeStruct(cache.shape, cache.dtype),
+        in_specs=[SMEM, SMEM, VMEM, ANY, ANY, ANY, ANY, ANY],
+        out_specs=ANY,
         scratch_shapes=[
             pltpu.VMEM(cache.shape, cache.dtype),
             pltpu.SemaphoreType.DMA((P_DEV, 2, SPLIT)),
@@ -375,45 +426,58 @@
         ],
         compiler_params=pltpu.CompilerParams(vmem_limit_bytes=16 << 20),
         name="assemble",
-    )(ancestors, lengths, logits, new_kv, cache, right1, left1, right2, left2)
-
-
-def crowded(ancestors):
-    source = ancestors // P_DEV
-    offset = source - jnp.arange(ancestors.shape[0], dtype=jnp.int32) // P_DEV
-    found = jnp.bool_(False)
-    for ahead in range(1, 2 * P_DEV):
-        here, there = slice(None, -ahead), slice(ahead, None)
-        both = (source[here] == source[there]) & (ancestors[here] != ancestors[there])
-        right = (offset[here] == -1) & (offset[there] == -2)
-        left = (offset[here] == 2) & (offset[there] == 1)
-        found = found | jnp.any(both & (right | left))
-    return found
+    )(ancestors, lengths, new_kv, cache, even1, odd1, even2, odd2)
+
+
+def normalize_kernel(logits, log_weight):
+    every = logits[...]
+    every = jnp.where(lax.broadcasted_iota(jnp.int32, every.shape, 2) < P_DEV, every, -jnp.inf)
+    peak = jnp.max(jnp.max(every, axis=0), axis=1, keepdims=True)
+    total = jnp.sum(jnp.sum(jnp.exp(every - peak), axis=0), axis=1, keepdims=True)
+    mine = logits[lax.axis_index("dom")] - (peak + jnp.log(total))
+    for slot in range(P_DEV):
+        log_weight[slot] = mine[0, slot]
+
+
+def normalize(logits):
+    return pl.pallas_call(
+        normalize_kernel,
+        out_shape=jax.ShapeDtypeStruct((P_DEV,), jnp.float32),
+        in_specs=[VMEM],
+        out_specs=SMEM,
+        compiler_params=pltpu.CompilerParams(vmem_limit_bytes=8 << 20),
+        name="normalize",
+    )(logits)
 
 
 def local(query, new_kv, cache, lengths, prior_logw, ancestors, w_reward):
-    right0, left0 = pack(ancestors, lengths, new_kv, cache, far=False)
-    right1 = shifted(right0, "dom", 1)
-    left1 = shifted(left0, "dom", -1)
-    heads = lax.all_to_all(spread_query(query), "tp", 0, 0)
+    even0, odd0, rows, flag = pack(ancestors, lengths, query, new_kv, cache)
+    even1 = swapped(even0, "dom", 0)
+    odd1 = swapped(odd0, "dom", 1)
+    heads = lax.all_to_all(rows, "tp", 0, 0)
     parts = attend(lengths, heads, new_kv, cache)
     parts = lax.all_to_all(parts, "tp", 0, 0)
-    parts, right1, left1 = lax.optimization_barrier((parts, right1, left1))
-    right2 = shifted(right1, "dom", 1)
-    left2 = shifted(left1, "dom", -1)
     weight = w_reward.astype(jnp.float32).reshape(HQ, HD)
+    parts, even1, odd1 = lax.optimization_barrier((parts, even1, odd1))
+    even2 = swapped(odd1, "dom", 0)
+    odd2 = swapped(even1, "dom", 1)
     attn, logits = merge(prior_logw, parts, weight, query.shape[1], lax.axis_size("dom"))
     logits = lax.all_to_all(logits, "dom", 0, 0)
 
-    def near(right2, left2):
-        return assemble(ancestors, lengths, logits, new_kv, cache, right1, left1, right2, left2)
-
-    def direct(right2, left2):
-        right0, left0 = pack(ancestors, lengths, new_kv, cache, far=True)
-        return near(shifted(right0, "dom", REACH), shifted(left0, "dom", -REACH))
-
-    new_cache, log_weight = lax.cond(crowded(ancestors), direct, near, right2, left2)
-    return (attn, log_weight, new_cache)
+    def near(even2, odd2):
+        return assemble(ancestors, lengths, new_kv, cache, even1, odd1, even2, odd2, far=False)
+
+    def direct(even2, odd2):
+        right0, left0 = pack_far(ancestors, lengths, new_kv, cache)
+        from_left = shifted(right0, "dom", REACH)
+        from_right = shifted(left0, "dom", -REACH)
+        return assemble(
+            ancestors, lengths, new_kv, cache, even1, odd1, from_right, from_left, far=True
+        )
+
+    new_cache = lax.cond(flag[0] > 0, direct, near, even2, odd2)
+    new_cache, logits = lax.optimization_barrier((new_cache, logits))
+    return (attn, normalize(logits), new_cache)
 
 
 def solution(mesh):

time: 83.6 us -> 78.3 us (0.937)
  the two profiles are of different devices: /device:TPU:8 before, /device:TPU:38 now
where the time goes in v2:
time: 78.3 us; the launch traced here: 77.9 us
  starting transfers between devices  31.6 us (40%)
  blocking collectives  18.6 us (24%)
  waiting for transfers between devices  15.8 us (20%)
  Pallas kernels  9.8 us (13%)
  between operations  1.42 us (2%)
    ppermute x4, starting transfers between devices, swapped(): return lax.ppermute(value, axis, pairs)  22.3 us
    ppermute x4, waiting for transfers between devices, swapped(): return lax.ppermute(value, axis, pairs)  15.8 us
    all_to_all x1, blocking collectives, local(): parts = lax.all_to_all(parts, 'tp', 0, 0)  10.6 us
    all_to_all x1, starting transfers between devices, local(): logits = lax.all_to_all(logits, 'dom', 0, 0)  9.31 us
    all_to_all x1, blocking collectives, local(): heads = lax.all_to_all(rows, 'tp', 0, 0)  7.95 us
    pallas_call x1, Pallas kernels, pack(): pl.pallas_call(pack_kernel, out_shape=(unit, unit, jax.ShapeDtypeStruct((...  3 us
    pallas_call x1, Pallas kernels, assemble(): pl.pallas_call(functools.partial(assemble_kernel, far), out_shape=jax.Sha...  2.91 us
  transfers between devices with their start and end apart: 5, of which 3 were waited for; matrix products, arithmetic and copies ran while one was open for 0% of the time, Pallas kernels for 8%

profile of v2, /device:TPU:38, one launch (start us, length us, event | category | flops | bytes accessed | tf_op | source)
XLA Modules:
  0.0 77.9 jit_solution(9320605009461999696)
XLA Ops:
  0.6 0.0 copy-start.5
  0.6 0.0 copy-start
  0.7 0.7 copy-done
  1.3 0.0 copy-start.2
  1.3 0.0 copy-start.3
  1.3 3.0 %pack.1 = (bf16[2,512,512]{2,1,0:T(8,128)(2,1)S(1)}, bf16[2,512,512]{2,1,0:T(8,128)(2,1)S(1)}, f32[8,8,128]{2,1,0:T(8,128)S(1)}, s32[1]{0:T(128)}) custom-call(s32[128]{0:T(128)} %ancestors.1, s32[2]{0:T(128)} %lengths.3, s32[1,128]{1,0:T(1,128)} %bitcast.5, bf16[2,448]{1,0:T(2,128)(2,1)S(1)} %copy-done, bf16[2,2,512]{2,1,0:T(2,128)(2,1)} %new_kv.3, ...), custom_call_target="tpu_custom_call" | custom-call | tf_op jit(solution)/shard_map/pack/pallas_call | solution.py:132
  4.3 0.0 copy-start.6
  4.4 0.0 copy-start.1
  4.4 0.0 copy-start.4
  4.4 4.5 %collective-permute-start.2 = (bf16[2,512,512]{2,1,0:T(8,128)(2,1)S(1)}, bf16[2,512,512]{2,1,0:T(8,128)(2,1)S(1)}, u32[]{:S(2)}, u32[]{:S(2)}) collective-permute-start(bf16[2,512,512]{2,1,0:T(8,128)(2,1)S(1)} %get-tuple-element.62), channel_id=1, source_target_pairs={{0,8},{8,0},{16,24},{24,16},{32,40},{40,32},{48,56},{56,48},{64,72... | collective-permute-start | bytes 3145736 | tf_op jit(solution)/shard_map/ppermute | solution.py:43
  8.9 8.9 %collective-permute-start.3 = (bf16[2,512,512]{2,1,0:T(8,128)(2,1)S(1)}, bf16[2,512,512]{2,1,0:T(8,128)(2,1)}, u32[]{:S(2)}, u32[]{:S(2)}) collective-permute-start(bf16[2,512,512]{2,1,0:T(8,128)(2,1)S(1)} %get-tuple-element.63), channel_id=1, source_target_pairs={{8,16},{16,8},{24,32},{32,24},{40,48},{48,40},{56,64},{64,56},{72,... | collective-permute-start | bytes 3145736 | tf_op jit(solution)/shard_map/ppermute | solution.py:43
  17.8 8.0 %all_to_all.15.heads = f32[8,8,128]{2,1,0:T(8,128)S(1)} all-to-all(f32[8,8,128]{2,1,0:T(8,128)S(1)} %get-tuple-element.61), channel_id=1, replica_groups=mesh['dom'=64,'tp'=8] {'tp'}, dimensions={0} | all-to-all | bytes 65536 | tf_op jit(solution)/shard_map/all_to_all | solution.py:457
  25.8 0.0 copy-done.5
  25.8 0.0 copy-done.2
  25.8 0.0 copy-done.3
  25.8 1.5 %attend.1 = f32[8,80,128]{2,1,0:T(8,128)S(1)} custom-call(s32[2]{0:T(128)S(1)} %copy-done.5, f32[8,8,128]{2,1,0:T(8,128)S(1)} %all_to_all.15.heads, bf16[2,2,512]{2,1,0:T(2,128)(2,1)S(1)} %copy-done.3, bf16[2,2,512,512]{3,2,1,0:T(8,128)(2,1)S(1)} %copy-done.2), custom_call_target="tpu_custom_call" | custom-call | tf_op jit(solution)/shard_map/attend/pallas_call | solution.py:271
  27.2 10.6 %all_to_all.16.parts = f32[8,80,128]{2,1,0:T(8,128)S(1)} all-to-all(f32[8,80,128]{2,1,0:T(8,128)S(1)} %attend.1), channel_id=1, replica_groups=mesh['dom'=64,'tp'=8] {'tp'}, dimensions={0} | all-to-all | bytes 655360 | tf_op jit(solution)/shard_map/all_to_all | solution.py:459
  37.8 0.0 collective-permute-done.2
  37.9 2.9 %collective-permute-done.3 = bf16[2,512,512]{2,1,0:T(8,128)(2,1)} collective-permute-done((bf16[2,512,512]{2,1,0:T(8,128)(2,1)S(1)}, bf16[2,512,512]{2,1,0:T(8,128)(2,1)}, u32[]{:S(2)}, u32[]{:S(2)}) %collective-permute-start.3) | collective-permute-done | bytes 1048608 | tf_op jit(solution)/shard_map/ppermute | solution.py:43
  40.8 7.0 %collective-permute-start.5 = (bf16[2,512,512]{2,1,0:T(8,128)(2,1)S(1)}, bf16[2,512,512]{2,1,0:T(8,128)(2,1)}, u32[]{:S(2)}, u32[]{:S(2)}) collective-permute-start(bf16[2,512,512]{2,1,0:T(8,128)(2,1)S(1)} %collective-permute-done.2), channel_id=1, source_target_pairs={{8,16},{16,8},{24,32},{32,24},{40,48},{48,40},{56,64},{64,56},{72,... | collective-permute-start | bytes 3145736 | tf_op jit(solution)/shard_map/ppermute | solution.py:43
  47.7 1.9 %collective-permute-start.4 = (bf16[2,512,512]{2,1,0:T(8,128)(2,1)}, bf16[2,512,512]{2,1,0:T(8,128)(2,1)}, u32[]{:S(2)}, u32[]{:S(2)}) collective-permute-start(bf16[2,512,512]{2,1,0:T(8,128)(2,1)} %collective-permute-done.3), channel_id=1, source_target_pairs={{0,8},{8,0},{16,24},{24,16},{32,40},{40,32},{48,56},{56,48},{64,72... | collective-permute-start | bytes 3145736 | tf_op jit(solution)/shard_map/ppermute | solution.py:43
  49.7 0.0 copy-done.6
  49.7 0.0 copy-done.1
  49.7 1.5 %merge.1 = (bf16[2,448]{1,0:T(2,128)(2,1)}, f32[64,1,128]{2,1,0:T(1,128)}) custom-call(f32[2]{0:T(128)S(1)} %copy-done.1, f32[8,80,128]{2,1,0:T(8,128)S(1)} %all_to_all.16.parts, f32[28,128]{1,0:T(8,128)S(1)} %bitcast_convert_fusion.weight), custom_call_target="tpu_custom_call" | custom-call | tf_op jit(solution)/shard_map/merge/pallas_call | solution.py:336
  51.2 9.3 %all-to-all-start.2 = ((f32[64,1,128]{2,1,0:T(1,128)}), f32[64,1,128]{2,1,0:T(1,128)S(1)}, u32[]{:S(2)}, u32[]{:S(2)}) async-start(f32[64,1,128]{2,1,0:T(1,128)} %get-tuple-element.69), calls=%async_computation.2 | async-start | bytes 65536 | tf_op jit(solution)/shard_map/all_to_all | solution.py:465
  61.2 9.7 %collective-permute-done.5 = bf16[2,512,512]{2,1,0:T(8,128)(2,1)} collective-permute-done((bf16[2,512,512]{2,1,0:T(8,128)(2,1)S(1)}, bf16[2,512,512]{2,1,0:T(8,128)(2,1)}, u32[]{:S(2)}, u32[]{:S(2)}) %collective-permute-start.5) | collective-permute-done | bytes 1048608 | tf_op jit(solution)/shard_map/ppermute | solution.py:43
  70.9 3.2 %collective-permute-done.4 = bf16[2,512,512]{2,1,0:T(8,128)(2,1)} collective-permute-done((bf16[2,512,512]{2,1,0:T(8,128)(2,1)}, bf16[2,512,512]{2,1,0:T(8,128)(2,1)}, u32[]{:S(2)}, u32[]{:S(2)}) %collective-permute-start.4) | collective-permute-done | bytes 1048608 | tf_op jit(solution)/shard_map/ppermute | solution.py:43
  74.1 0.0 copy-done.4
  74.1 2.9 %conditional.1 = (bf16[2,2,512,512]{3,2,1,0:T(8,128)(2,1)}) conditional(s32[]{:T(128)} %bitcast.2, (s32[128]{0:T(128)S(1)}, s32[2]{0:T(128)S(1)}, bf16[2,2,512]{2,1,0:T(2,128)(2,1)S(1)}, bf16[2,2,512,512]{3,2,1,0:T(8,128)(2,1)S(1)}, bf16[2,512,512]{2,1,0:T(8,128)(2,1)S(1)}, /*index=5*/bf16[2,512,512]{2,1,0:T(8,128)(2,1)}, ...), branch_computations={%region_0.0_spmd, %region_1.0_spmd} | conditional | bytes 8388696 | solution.py:478
  74.1 2.9 %assemble.2 = bf16[2,2,512,512]{3,2,1,0:T(8,128)(2,1)} custom-call(s32[128]{0:T(128)S(1)} %get-tuple-element.21.ancestors, s32[2]{0:T(128)S(1)} %get-tuple-element.32.lengths, bf16[2,2,512]{2,1,0:T(2,128)(2,1)S(1)} %get-tuple-element.33.new_kv, bf16[2,2,512,512]{3,2,1,0:T(8,128)(2,1)S(1)} %get-tuple-element.34.cache, ...), custom_call_target="tpu_custom_call" | custom-call | tf_op jit(solution)/shard_map/cond/branch_0_fun/assemble/pallas_call | solution.py:417
  77.0 0.0 all-to-all-done.2.logits
  77.0 0.9 %normalize.1 = f32[2]{0:T(128)} custom-call(f32[64,1,128]{2,1,0:T(1,128)S(1)} %all-to-all-done.2.logits), custom_call_target="tpu_custom_call" | custom-call | tf_op jit(solution)/shard_map/normalize/pallas_call | solution.py:443
  (1 shorter events, 0.0 us)
Async XLA Ops:
  0.6 25.1 %copy-start.5 = (s32[2]{0:T(128)S(1)}, s32[2]{0:T(128)}, u32[]{:S(2)}) copy-start(s32[2]{0:T(128)} %lengths.3) | copy-start | bytes 28
  0.6 0.7 copy-start
  1.3 24.4 %copy-start.2 = (bf16[2,2,512,512]{3,2,1,0:T(8,128)(2,1)S(1)}, bf16[2,2,512,512]{3,2,1,0:T(8,128)(2,1)}, u32[]{:S(2)}) copy-start(bf16[2,2,512,512]{3,2,1,0:T(8,128)(2,1)} %kv.1) | copy-start | bytes 6291460
  1.3 24.4 %copy-start.3 = (bf16[2,2,512]{2,1,0:T(2,128)(2,1)S(1)}, bf16[2,2,512]{2,1,0:T(2,128)(2,1)}, u32[]{:S(2)}) copy-start(bf16[2,2,512]{2,1,0:T(2,128)(2,1)} %new_kv.3) | copy-start | bytes 12292
  4.3 45.3 %copy-start.6 = (bf16[3584]{0:T(1024)(128)(2,1)S(1)}, bf16[3584]{0:T(1024)(128)(2,1)}, u32[]{:S(2)}) copy-start(bf16[3584]{0:T(1024)(128)(2,1)} %param.15) | copy-start | bytes 21508
  4.4 45.3 %copy-start.1 = (f32[2]{0:T(128)S(1)}, f32[2]{0:T(128)}, u32[]{:S(2)}) copy-start(f32[2]{0:T(128)} %prior.1) | copy-start | bytes 28
  4.4 69.7 %copy-start.4 = (s32[128]{0:T(128)S(1)}, s32[128]{0:T(128)}, u32[]{:S(2)}) copy-start(s32[128]{0:T(128)} %ancestors.1) | copy-start | bytes 1540
  4.4 33.5 %collective-permute-start.2 = (bf16[2,512,512]{2,1,0:T(8,128)(2,1)S(1)}, bf16[2,512,512]{2,1,0:T(8,128)(2,1)S(1)}, u32[]{:S(2)}, u32[]{:S(2)}) collective-permute-start(bf16[2,512,512]{2,1,0:T(8,128)(2,1)S(1)} %get-tuple-element.62), channel_id=1, source_target_pairs={{0,8},{8,0},{16,24},{24,16},{32,40},{40,32},{48,56},{56,48},{64,72... | collective-permute-start | bytes 3145736 | tf_op jit(solution)/shard_map/ppermute | solution.py:43
  8.9 31.9 %collective-permute-start.3 = (bf16[2,512,512]{2,1,0:T(8,128)(2,1)S(1)}, bf16[2,512,512]{2,1,0:T(8,128)(2,1)}, u32[]{:S(2)}, u32[]{:S(2)}) collective-permute-start(bf16[2,512,512]{2,1,0:T(8,128)(2,1)S(1)} %get-tuple-element.63), channel_id=1, source_target_pairs={{8,16},{16,8},{24,32},{32,24},{40,48},{48,40},{56,64},{64,56},{72,... | collective-permute-start | bytes 3145736 | tf_op jit(solution)/shard_map/ppermute | solution.py:43
  40.8 30.1 %collective-permute-start.5 = (bf16[2,512,512]{2,1,0:T(8,128)(2,1)S(1)}, bf16[2,512,512]{2,1,0:T(8,128)(2,1)}, u32[]{:S(2)}, u32[]{:S(2)}) collective-permute-start(bf16[2,512,512]{2,1,0:T(8,128)(2,1)S(1)} %collective-permute-done.2), channel_id=1, source_target_pairs={{8,16},{16,8},{24,32},{32,24},{40,48},{48,40},{56,64},{64,56},{72,... | collective-permute-start | bytes 3145736 | tf_op jit(solution)/shard_map/ppermute | solution.py:43
  47.7 26.3 %collective-permute-start.4 = (bf16[2,512,512]{2,1,0:T(8,128)(2,1)}, bf16[2,512,512]{2,1,0:T(8,128)(2,1)}, u32[]{:S(2)}, u32[]{:S(2)}) collective-permute-start(bf16[2,512,512]{2,1,0:T(8,128)(2,1)} %collective-permute-done.3), channel_id=1, source_target_pairs={{0,8},{8,0},{16,24},{24,16},{32,40},{40,32},{48,56},{56,48},{64,72... | collective-permute-start | bytes 3145736 | tf_op jit(solution)/shard_map/ppermute | solution.py:43
  51.2 25.8 %all-to-all-start.2 = ((f32[64,1,128]{2,1,0:T(1,128)}), f32[64,1,128]{2,1,0:T(1,128)S(1)}, u32[]{:S(2)}, u32[]{:S(2)}) async-start(f32[64,1,128]{2,1,0:T(1,128)} %get-tuple-element.69), calls=%async_computation.2 | async-start | bytes 65536 | tf_op jit(solution)/shard_map/all_to_all | solution.py:465

commit v3 on v2

--- a/solution.py
+++ b/solution.py
@@ -347,6 +347,7 @@
             pltpu.VMEM((8, OWN * HD), jnp.float32),
         ],
         compiler_params=pltpu.CompilerParams(vmem_limit_bytes=8 << 20),
+        cost_estimate=pl.CostEstimate(flops=10**11, bytes_accessed=10**9, transcendentals=0),
         name="merge",
     )(prior, parts, weight)
 
@@ -456,11 +457,13 @@
     odd1 = swapped(odd0, "dom", 1)
     heads = lax.all_to_all(rows, "tp", 0, 0)
     parts = attend(lengths, heads, new_kv, cache)
+    weight = w_reward.astype(jnp.float32).reshape(HQ, HD)
+    sent = parts
     parts = lax.all_to_all(parts, "tp", 0, 0)
-    weight = w_reward.astype(jnp.float32).reshape(HQ, HD)
-    parts, even1, odd1 = lax.optimization_barrier((parts, even1, odd1))
+    even1, sent = lax.optimization_barrier((even1, sent))
+    odd2 = swapped(even1, "dom", 1)
+    odd1, sent = lax.optimization_barrier((odd1, sent))
     even2 = swapped(odd1, "dom", 0)
-    odd2 = swapped(even1, "dom", 1)
     attn, logits = merge(prior_logw, parts, weight, query.shape[1], lax.axis_size("dom"))
     logits = lax.all_to_all(logits, "dom", 0, 0)
 

time: 78.3 us -> 73.9 us (0.944)
  the two profiles are of different devices: /device:TPU:38 before, /device:TPU:46 now
where the time goes in v3:
time: 73.9 us; the launch traced here: 73.4 us
  starting transfers between devices  40.6 us (55%)
  waiting for transfers between devices  12.2 us (17%)
  Pallas kernels  10.5 us (14%)
  blocking collectives  7.94 us (11%)
  between operations  1.43 us (2%)
    ppermute x4, starting transfers between devices, swapped(): return lax.ppermute(value, axis, pairs)  24.9 us
    ppermute x4, waiting for transfers between devices, swapped(): return lax.ppermute(value, axis, pairs)  12.2 us
    all_to_all x1, starting transfers between devices, local(): logits = lax.all_to_all(logits, 'dom', 0, 0)  10.3 us
    all_to_all x1, blocking collectives, local(): heads = lax.all_to_all(rows, 'tp', 0, 0)  7.94 us
    all_to_all x1, starting transfers between devices, local(): parts = lax.all_to_all(parts, 'tp', 0, 0)  5.44 us
    pallas_call x1, Pallas kernels, assemble(): pl.pallas_call(functools.partial(assemble_kernel, far), out_shape=jax.Sha...  2.95 us
    pallas_call x1, Pallas kernels, pack(): pl.pallas_call(pack_kernel, out_shape=(unit, unit, jax.ShapeDtypeStruct((...  2.93 us
    pallas_call x1, Pallas kernels, attend(): pl.pallas_call(attend_kernel, out_shape=jax.ShapeDtypeStruct((TP, P_DEV *...  2.19 us
  transfers between devices with their start and end apart: 6, of which 2 were waited for; matrix products, arithmetic and copies ran while one was open for 0% of the time, Pallas kernels for 9%

profile of v3, /device:TPU:46, one launch (start us, length us, event | category | flops | bytes accessed | tf_op | source)
XLA Modules:
  0.0 73.4 jit_solution(2965874816149062454)
XLA Ops:
  0.6 0.0 copy-start.6
  0.6 0.0 copy-start
  0.7 0.7 copy-done
  1.3 0.0 copy-start.2
  1.3 0.0 copy-start.4
  1.3 2.9 %pack.1 = (bf16[2,512,512]{2,1,0:T(8,128)(2,1)S(1)}, bf16[2,512,512]{2,1,0:T(8,128)(2,1)S(1)}, f32[8,8,128]{2,1,0:T(8,128)S(1)}, s32[1]{0:T(128)}) custom-call(s32[128]{0:T(128)} %ancestors.1, s32[2]{0:T(128)} %lengths.3, s32[1,128]{1,0:T(1,128)} %bitcast.5, bf16[2,448]{1,0:T(2,128)(2,1)S(1)} %copy-done, bf16[2,2,512]{2,1,0:T(2,128)(2,1)} %new_kv.3, ...), custom_call_target="tpu_custom_call" | custom-call | tf_op jit(solution)/shard_map/pack/pallas_call | solution.py:132
  4.3 0.0 copy-start.7
  4.3 0.0 copy-start.1
  4.3 4.3 %collective-permute-start.2 = (bf16[2,512,512]{2,1,0:T(8,128)(2,1)S(1)}, bf16[2,512,512]{2,1,0:T(8,128)(2,1)S(1)}, u32[]{:S(2)}, u32[]{:S(2)}) collective-permute-start(bf16[2,512,512]{2,1,0:T(8,128)(2,1)S(1)} %get-tuple-element.62), channel_id=1, source_target_pairs={{0,8},{8,0},{16,24},{24,16},{32,40},{40,32},{48,56},{56,48},{64,72... | collective-permute-start | bytes 3145736 | tf_op jit(solution)/shard_map/ppermute | solution.py:43
  8.6 9.9 %collective-permute-start.3 = (bf16[2,512,512]{2,1,0:T(8,128)(2,1)S(1)}, bf16[2,512,512]{2,1,0:T(8,128)(2,1)}, u32[]{:S(2)}, u32[]{:S(2)}) collective-permute-start(bf16[2,512,512]{2,1,0:T(8,128)(2,1)S(1)} %get-tuple-element.64), channel_id=1, source_target_pairs={{8,16},{16,8},{24,32},{32,24},{40,48},{48,40},{56,64},{64,56},{72,... | collective-permute-start | bytes 3145736 | tf_op jit(solution)/shard_map/ppermute | solution.py:43
  18.5 7.9 %all_to_all.15.heads = f32[8,8,128]{2,1,0:T(8,128)S(1)} all-to-all(f32[8,8,128]{2,1,0:T(8,128)S(1)} %get-tuple-element.59), channel_id=1, replica_groups=mesh['dom'=64,'tp'=8] {'tp'}, dimensions={0} | all-to-all | bytes 65536 | tf_op jit(solution)/shard_map/all_to_all | solution.py:458
  26.5 0.0 copy-done.6
  26.5 0.0 copy-done.2
  26.5 0.0 copy-done.4
  26.5 2.2 %attend.1 = f32[8,80,128]{2,1,0:T(8,128)} custom-call(s32[2]{0:T(128)S(1)} %copy-done.6, f32[8,8,128]{2,1,0:T(8,128)S(1)} %all_to_all.15.heads, bf16[2,2,512]{2,1,0:T(2,128)(2,1)S(1)} %copy-done.4, bf16[2,2,512,512]{3,2,1,0:T(8,128)(2,1)S(1)} %copy-done.2), custom_call_target="tpu_custom_call" | custom-call | tf_op jit(solution)/shard_map/attend/pallas_call | solution.py:271
  28.7 5.4 %all-to-all-start.1 = ((f32[8,80,128]{2,1,0:T(8,128)}), f32[8,80,128]{2,1,0:T(8,128)S(1)}, u32[]{:S(2)}, u32[]{:S(2)}) async-start(f32[8,80,128]{2,1,0:T(8,128)} %attend.1), calls=%async_computation.1 | async-start | bytes 655360 | tf_op jit(solution)/shard_map/all_to_all | solution.py:462
  34.1 0.0 copy-done.7
  34.1 0.0 copy-start.5
  34.1 0.0 collective-permute-done.2
  34.1 8.7 %collective-permute-start.5 = (bf16[2,512,512]{2,1,0:T(8,128)(2,1)S(1)}, bf16[2,512,512]{2,1,0:T(8,128)(2,1)S(1)}, u32[]{:S(2)}, u32[]{:S(2)}) collective-permute-start(bf16[2,512,512]{2,1,0:T(8,128)(2,1)S(1)} %collective-permute-done.2), channel_id=1, source_target_pairs={{8,16},{16,8},{24,32},{32,24},{40,48},{48,40},{56,64},{64,56},{72,... | collective-permute-start | bytes 3145736 | tf_op jit(solution)/shard_map/ppermute | solution.py:43
  42.9 0.0 collective-permute-done.3
  42.9 1.9 %collective-permute-start.4 = (bf16[2,512,512]{2,1,0:T(8,128)(2,1)}, bf16[2,512,512]{2,1,0:T(8,128)(2,1)S(1)}, u32[]{:S(2)}, u32[]{:S(2)}) collective-permute-start(bf16[2,512,512]{2,1,0:T(8,128)(2,1)} %collective-permute-done.3), channel_id=1, source_target_pairs={{0,8},{8,0},{16,24},{24,16},{32,40},{40,32},{48,56},{56,48},{64,72... | collective-permute-start | bytes 3145736 | tf_op jit(solution)/shard_map/ppermute | solution.py:43
  44.8 0.0 all-to-all-done.1.parts
  44.8 0.0 copy-done.1
  44.8 1.5 %merge.1 = (bf16[2,448]{1,0:T(2,128)(2,1)}, f32[64,1,128]{2,1,0:T(1,128)}) custom-call(f32[2]{0:T(128)S(1)} %copy-done.1, f32[8,80,128]{2,1,0:T(8,128)S(1)} %all-to-all-done.1.parts, f32[28,128]{1,0:T(8,128)S(1)} %bitcast_convert_fusion.weight), custom_call_target="tpu_custom_call" | custom-call | flops 99999997952 | bytes 1000000000 | tf_op jit(solution)/shard_map/merge/pallas_call | solution.py:336
  46.4 10.3 %all-to-all-start.2 = ((f32[64,1,128]{2,1,0:T(1,128)}), f32[64,1,128]{2,1,0:T(1,128)S(1)}, u32[]{:S(2)}, u32[]{:S(2)}) async-start(f32[64,1,128]{2,1,0:T(1,128)} %get-tuple-element.65), calls=%async_computation.2 | async-start | bytes 65536 | tf_op jit(solution)/shard_map/all_to_all | solution.py:468
  57.3 8.8 %collective-permute-done.5 = bf16[2,512,512]{2,1,0:T(8,128)(2,1)S(1)} collective-permute-done((bf16[2,512,512]{2,1,0:T(8,128)(2,1)S(1)}, bf16[2,512,512]{2,1,0:T(8,128)(2,1)S(1)}, u32[]{:S(2)}, u32[]{:S(2)}) %collective-permute-start.5) | collective-permute-done | bytes 1048608 | tf_op jit(solution)/shard_map/ppermute | solution.py:43
  66.2 3.3 %collective-permute-done.4 = bf16[2,512,512]{2,1,0:T(8,128)(2,1)S(1)} collective-permute-done((bf16[2,512,512]{2,1,0:T(8,128)(2,1)}, bf16[2,512,512]{2,1,0:T(8,128)(2,1)S(1)}, u32[]{:S(2)}, u32[]{:S(2)}) %collective-permute-start.4) | collective-permute-done | bytes 1048608 | tf_op jit(solution)/shard_map/ppermute | solution.py:43
  69.5 0.0 copy-done.5
  69.5 3.0 %conditional.1 = (bf16[2,2,512,512]{3,2,1,0:T(8,128)(2,1)}) conditional(s32[]{:T(128)} %bitcast.2, (s32[128]{0:T(128)S(1)}, s32[2]{0:T(128)S(1)}, bf16[2,2,512]{2,1,0:T(2,128)(2,1)S(1)}, bf16[2,2,512,512]{3,2,1,0:T(8,128)(2,1)}, bf16[2,512,512]{2,1,0:T(8,128)(2,1)S(1)}, /*index=5*/bf16[2,512,512]{2,1,0:T(8,128)(2,1)}, ...), branch_computations={%region_0.0_spmd, %region_1.0_spmd} | conditional | bytes 16777332 | solution.py:481
  69.5 3.0 %assemble.2 = bf16[2,2,512,512]{3,2,1,0:T(8,128)(2,1)} custom-call(s32[128]{0:T(128)S(1)} %get-tuple-element.21.ancestors, s32[2]{0:T(128)S(1)} %get-tuple-element.32.lengths, bf16[2,2,512]{2,1,0:T(2,128)(2,1)S(1)} %get-tuple-element.33.new_kv, bf16[2,2,512,512]{3,2,1,0:T(8,128)(2,1)} %get-tuple-element.34.cache, ...), custom_call_target="tpu_custom_call" | custom-call | tf_op jit(solution)/shard_map/cond/branch_0_fun/assemble/pallas_call | solution.py:418
  72.5 0.0 all-to-all-done.2.logits
  72.5 0.9 %normalize.1 = f32[2]{0:T(128)} custom-call(f32[64,1,128]{2,1,0:T(1,128)S(1)} %all-to-all-done.2.logits), custom_call_target="tpu_custom_call" | custom-call | tf_op jit(solution)/shard_map/normalize/pallas_call | solution.py:444
  (1 shorter events, 0.0 us)
Async XLA Ops:
  0.6 25.8 %copy-start.6 = (s32[2]{0:T(128)S(1)}, s32[2]{0:T(128)}, u32[]{:S(2)}) copy-start(s32[2]{0:T(128)} %lengths.3) | copy-start | bytes 28
  0.6 0.7 copy-start
  1.3 25.1 %copy-start.2 = (bf16[2,2,512,512]{3,2,1,0:T(8,128)(2,1)S(1)}, bf16[2,2,512,512]{3,2,1,0:T(8,128)(2,1)}, u32[]{:S(2)}) copy-start(bf16[2,2,512,512]{3,2,1,0:T(8,128)(2,1)} %kv.1) | copy-start | bytes 6291460
  1.3 25.1 %copy-start.4 = (bf16[2,2,512]{2,1,0:T(2,128)(2,1)S(1)}, bf16[2,2,512]{2,1,0:T(2,128)(2,1)}, u32[]{:S(2)}) copy-start(bf16[2,2,512]{2,1,0:T(2,128)(2,1)} %new_kv.3) | copy-start | bytes 12292
  4.3 29.8 %copy-start.7 = (bf16[3584]{0:T(1024)(128)(2,1)S(1)}, bf16[3584]{0:T(1024)(128)(2,1)}, u32[]{:S(2)}) copy-start(bf16[3584]{0:T(1024)(128)(2,1)} %param.15) | copy-start | bytes 21508
  4.3 40.5 %copy-start.1 = (f32[2]{0:T(128)S(1)}, f32[2]{0:T(128)}, u32[]{:S(2)}) copy-start(f32[2]{0:T(128)} %prior.1) | copy-start | bytes 28
  4.3 29.8 %collective-permute-start.2 = (bf16[2,512,512]{2,1,0:T(8,128)(2,1)S(1)}, bf16[2,512,512]{2,1,0:T(8,128)(2,1)S(1)}, u32[]{:S(2)}, u32[]{:S(2)}) collective-permute-start(bf16[2,512,512]{2,1,0:T(8,128)(2,1)S(1)} %get-tuple-element.62), channel_id=1, source_target_pairs={{0,8},{8,0},{16,24},{24,16},{32,40},{40,32},{48,56},{56,48},{64,72... | collective-permute-start | bytes 3145736 | tf_op jit(solution)/shard_map/ppermute | solution.py:43
  8.6 34.2 %collective-permute-start.3 = (bf16[2,512,512]{2,1,0:T(8,128)(2,1)S(1)}, bf16[2,512,512]{2,1,0:T(8,128)(2,1)}, u32[]{:S(2)}, u32[]{:S(2)}) collective-permute-start(bf16[2,512,512]{2,1,0:T(8,128)(2,1)S(1)} %get-tuple-element.64), channel_id=1, source_target_pairs={{8,16},{16,8},{24,32},{32,24},{40,48},{48,40},{56,64},{64,56},{72,... | collective-permute-start | bytes 3145736 | tf_op jit(solution)/shard_map/ppermute | solution.py:43
  28.7 16.2 %all-to-all-start.1 = ((f32[8,80,128]{2,1,0:T(8,128)}), f32[8,80,128]{2,1,0:T(8,128)S(1)}, u32[]{:S(2)}, u32[]{:S(2)}) async-start(f32[8,80,128]{2,1,0:T(8,128)} %attend.1), calls=%async_computation.1 | async-start | bytes 655360 | tf_op jit(solution)/shard_map/all_to_all | solution.py:462
  34.1 35.4 %copy-start.5 = (s32[128]{0:T(128)S(1)}, s32[128]{0:T(128)}, u32[]{:S(2)}) copy-start(s32[128]{0:T(128)} %ancestors.1) | copy-start | bytes 1540
  34.1 32.0 %collective-permute-start.5 = (bf16[2,512,512]{2,1,0:T(8,128)(2,1)S(1)}, bf16[2,512,512]{2,1,0:T(8,128)(2,1)S(1)}, u32[]{:S(2)}, u32[]{:S(2)}) collective-permute-start(bf16[2,512,512]{2,1,0:T(8,128)(2,1)S(1)} %collective-permute-done.2), channel_id=1, source_target_pairs={{8,16},{16,8},{24,32},{32,24},{40,48},{48,40},{56,64},{64,56},{72,... | collective-permute-start | bytes 3145736 | tf_op jit(solution)/shard_map/ppermute | solution.py:43
  42.9 26.6 %collective-permute-start.4 = (bf16[2,512,512]{2,1,0:T(8,128)(2,1)}, bf16[2,512,512]{2,1,0:T(8,128)(2,1)S(1)}, u32[]{:S(2)}, u32[]{:S(2)}) collective-permute-start(bf16[2,512,512]{2,1,0:T(8,128)(2,1)} %collective-permute-done.3), channel_id=1, source_target_pairs={{0,8},{8,0},{16,24},{24,16},{32,40},{40,32},{48,56},{56,48},{64,72... | collective-permute-start | bytes 3145736 | tf_op jit(solution)/shard_map/ppermute | solution.py:43
  46.4 26.1 %all-to-all-start.2 = ((f32[64,1,128]{2,1,0:T(1,128)}), f32[64,1,128]{2,1,0:T(1,128)S(1)}, u32[]{:S(2)}, u32[]{:S(2)}) async-start(f32[64,1,128]{2,1,0:T(1,128)} %get-tuple-element.65), calls=%async_computation.2 | async-start | bytes 65536 | tf_op jit(solution)/shard_map/all_to_all | solution.py:468

commit v4 on v3

--- a/solution.py
+++ b/solution.py
@@ -79,7 +79,8 @@
     return (jnp.sum(found) > 0.0).astype(jnp.int32)
 
 
-def pad_query(query, out, wide):
+def spread_kernel(row, query, out, flag, wide):
+    flag[0] = crowded(row)
     columns = query.shape[1]
     wide[...] = jnp.zeros_like(wide)
     wide[0:P_DEV, 0:columns] = query[...].astype(jnp.float32)
@@ -93,95 +94,61 @@
                 out[receiver, pl.ds(OWN * particle + j, 1), :] = one
 
 
-def pack_kernel(
-    ancestors, lengths, row, query, new_kv, cache, even, odd, rows, flag, asked, fresh, wide, sems, small_sems
-):
+def spread(ancestors, query):
+    return pl.pallas_call(
+        spread_kernel,
+        out_shape=(
+            jax.ShapeDtypeStruct((TP, P_DEV * OWN, HD), jnp.float32),
+            jax.ShapeDtypeStruct((1,), jnp.int32),
+        ),
+        in_specs=[VMEM, VMEM],
+        out_specs=(VMEM, SMEM),
+        scratch_shapes=[pltpu.VMEM((8, OWN * HD), jnp.float32)],
+        compiler_params=pltpu.CompilerParams(vmem_limit_bytes=8 << 20),
+        name="spread",
+    )(ancestors.reshape(1, -1), query)
+
+
+def pack_kernel(far, ancestors, lengths, new_kv, cache, inner, outer, fresh, sems, small_sem):
     device = lax.axis_index("dom")
     length = cache.shape[2]
     first = lax.axis_index("tp") * length
-    small = [
-        pltpu.make_async_copy(query, asked, small_sems.at[0]),
-        pltpu.make_async_copy(new_kv, fresh, small_sems.at[1]),
-    ]
-    facing = 1 - 2 * (device & 1)
+    facing = 1 if far else 1 - 2 * (device & 1)
     units = []
-    for side, (out, sign) in enumerate(((even, facing), (odd, -facing))):
-        particle = pick(ancestors, device, [device + sign, device + 2 * sign])
-        for kv in range(2):
-            copy = pltpu.make_async_copy(cache.at[particle, kv], out.at[kv], sems.at[side, kv])
-            copy.start()
-            units.append((out, particle, kv, copy))
-    for copy in small:
+    for side, (out, sign) in enumerate(((inner, facing), (outer, -facing))):
+        receivers = [device + REACH * sign] if far else [device + sign, device + REACH * sign]
+        particle = pick(ancestors, device, receivers)
+        copy = pltpu.make_async_copy(cache.at[particle], out, sems.at[side])
         copy.start()
-    flag[0] = crowded(row)
-    for copy in small:
-        copy.wait()
-    pad_query(asked, rows, wide)
-    for out, particle, kv, copy in units:
+        units.append((out, particle, copy))
+    small = pltpu.make_async_copy(new_kv, fresh, small_sem)
+    small.start()
+    small.wait()
+    for out, particle, copy in units:
         copy.wait()
         position = lengths[particle]
 
         @pl.when((position >= first) & (position < first + length))
         def _():
             new = fresh[particle].astype(jnp.float32)
-            patch(out.at[kv], first, position, new[kv : kv + 1])
-
-
-def pack(ancestors, lengths, query, new_kv, cache):
+            for kv in range(2):
+                patch(out.at[kv], first, position, new[kv : kv + 1])
+
+
+def pack(ancestors, lengths, new_kv, cache, far):
     unit = jax.ShapeDtypeStruct(cache.shape[1:], cache.dtype)
     return pl.pallas_call(
-        pack_kernel,
-        out_shape=(
-            unit,
-            unit,
-            jax.ShapeDtypeStruct((TP, P_DEV * OWN, HD), jnp.float32),
-            jax.ShapeDtypeStruct((1,), jnp.int32),
-        ),
-        in_specs=[SMEM, SMEM, VMEM, HBM, HBM, HBM],
-        out_specs=(VMEM, VMEM, VMEM, SMEM),
+        functools.partial(pack_kernel, far),
+        out_shape=(unit, unit),
+        in_specs=[SMEM, SMEM, HBM, HBM],
+        out_specs=(VMEM, VMEM),
         scratch_shapes=[
-            pltpu.VMEM(query.shape, query.dtype),
             pltpu.VMEM(new_kv.shape, new_kv.dtype),
-            pltpu.VMEM((8, OWN * HD), jnp.float32),
-            pltpu.SemaphoreType.DMA((P_DEV, 2)),
             pltpu.SemaphoreType.DMA((2,)),
+            pltpu.SemaphoreType.DMA,
         ],
         compiler_params=pltpu.CompilerParams(vmem_limit_bytes=16 << 20),
-        name="pack",
-    )(ancestors, lengths, ancestors.reshape(1, -1), query, new_kv, cache)
-
-
-def pack_far_kernel(ancestors, lengths, new_kv, cache, right, left, sems):
-    device = lax.axis_index("dom")
-    length = cache.shape[2]
-    first = lax.axis_index("tp") * length
-    copies = []
-    for side, (out, sign) in enumerate(((right, 1), (left, -1))):
-        particle = pick(ancestors, device, [device + REACH * sign])
-        copy = pltpu.make_async_copy(cache.at[particle], out, sems.at[side])
-        copy.start()
-        copies.append((out, particle, copy))
-    for out, particle, copy in copies:
-        copy.wait()
-        position = lengths[particle]
-
-        @pl.when((position >= first) & (position < first + length))
-        def _():
-            fresh = new_kv[particle].astype(jnp.float32)
-            for kv in range(2):
-                patch(out.at[kv], first, position, fresh[kv : kv + 1])
-
-
-def pack_far(ancestors, lengths, new_kv, cache):
-    unit = jax.ShapeDtypeStruct(cache.shape[1:], cache.dtype)
-    return pl.pallas_call(
-        pack_far_kernel,
-        out_shape=(unit, unit),
-        in_specs=[SMEM, SMEM, VMEM, ANY],
-        out_specs=(VMEM, VMEM),
-        scratch_shapes=[pltpu.SemaphoreType.DMA((P_DEV,))],
-        compiler_params=pltpu.CompilerParams(vmem_limit_bytes=16 << 20),
-        name="pack_far",
+        name="pack_far" if far else "pack",
     )(ancestors, lengths, new_kv, cache)
 
 
@@ -352,82 +319,108 @@
     )(prior, parts, weight)
 
 
-SPLIT = 2
-
-
 def assemble_kernel(
-    far, ancestors, lengths, new_kv, cache, even1, odd1, even2, odd2, new_cache, buffer, in_sems, out_sems
+    ancestors, lengths, new_kv, cache, inner1, outer1, new_cache, buffer, in_sems, out_sems
 ):
     device = lax.axis_index("dom")
     length = cache.shape[2]
     first = lax.axis_index("tp") * length
-    rows = length // SPLIT
-    pieces = [
-        (slot, kv, part) for part in range(SPLIT) for kv in range(2) for slot in range(P_DEV)
-    ]
-    owner = [ancestors[P_DEV * device + slot] for slot in range(P_DEV)]
-
-    def arriving(ref, piece):
-        slot, kv, part = piece
-        at = pl.ds(part * rows, rows)
-        return pltpu.make_async_copy(ref.at[kv, at], buffer.at[slot, kv, at], in_sems.at[slot, kv, part])
-
-    for piece in pieces:
-        offset = (owner[piece[0]] >> 1) - device
+
+    def enter(ref, slot, kv):
+        return pltpu.make_async_copy(ref.at[kv], buffer.at[slot, kv], in_sems.at[slot, kv])
+
+    def leave(slot, kv):
+        return pltpu.make_async_copy(
+            buffer.at[slot, kv], new_cache.at[slot, kv], out_sems.at[slot, kv]
+        )
+
+    slots = []
+    for slot in range(P_DEV):
+        owner = ancestors[P_DEV * device + slot]
+        particle = owner & 1
+        offset = (owner >> 1) - device
         facing = offset * (1 - 2 * (device & 1))
-        two = offset if far else facing
-
-        @pl.when(offset == 0)
+        for found, ref in ((offset == 0, cache.at[particle]), (facing == 1, inner1), (facing == -1, outer1)):
+
+            @pl.when(found)
+            def _():
+                for kv in range(2):
+                    enter(ref, slot, kv).start()
+
+        row = lengths[particle]
+        patched = (offset == 0) & (row >= first) & (row < first + length)
+        slots.append((slot, particle, row, patched, jnp.abs(offset) <= 1))
+    for slot, particle, row, patched, near in slots:
+        for kv in range(2):
+
+            @pl.when(near)
+            def _():
+                enter(inner1, slot, kv).wait()
+
+            @pl.when(patched)
+            def _():
+                fresh = new_kv[particle].astype(jnp.float32)
+                patch(buffer.at[slot, kv], first, row, fresh[kv : kv + 1])
+
+            @pl.when(near)
+            def _():
+                leave(slot, kv).start()
+
+    for slot, particle, row, patched, near in slots:
+        for kv in range(2):
+
+            @pl.when(near)
+            def _():
+                leave(slot, kv).wait()
+
+
+def finish_kernel(far, ancestors, inner2, outer2, held, new_cache, sems):
+    device = lax.axis_index("dom")
+    slots = []
+    for slot in range(P_DEV):
+        offset = (ancestors[P_DEV * device + slot] >> 1) - device
+        side = offset if far else offset * (1 - 2 * (device & 1))
+        for found, ref in ((side == REACH, inner2), (side == -REACH, outer2)):
+
+            @pl.when(found)
+            def _():
+                pltpu.make_async_copy(ref, new_cache.at[slot], sems.at[slot]).start()
+
+        slots.append((slot, jnp.abs(offset) == REACH))
+    for slot, found in slots:
+
+        @pl.when(found)
         def _():
-            arriving(cache.at[owner[piece[0]] & 1], piece).start()
-
-        for found, ref in (
-            (facing == 1, even1),
-            (facing == -1, odd1),
-            (two == REACH, even2),
-            (two == -REACH, odd2),
-        ):
-
-            @pl.when(found)
-            def _():
-                arriving(ref, piece).start()
-
-    leaving = []
-    for piece in pieces:
-        slot, kv, part = piece
-        at = pl.ds(part * rows, rows)
-        arriving(even1, piece).wait()
-        particle = owner[slot] & 1
-        row = lengths[particle] - (first + part * rows)
-
-        @pl.when((owner[slot] >> 1 == device) & (row >= 0) & (row < rows))
-        def _():
-            fresh = new_kv[particle].astype(jnp.float32)
-            patch(buffer.at[slot, kv], 0, row + part * rows, fresh[kv : kv + 1])
-
-        copy = pltpu.make_async_copy(
-            buffer.at[slot, kv, at], new_cache.at[slot, kv, at], out_sems.at[slot, kv, part]
-        )
-        copy.start()
-        leaving.append(copy)
-    for copy in leaving:
-        copy.wait()
-
-
-def assemble(ancestors, lengths, new_kv, cache, even1, odd1, even2, odd2, far):
-    return pl.pallas_call(
-        functools.partial(assemble_kernel, far),
+            pltpu.make_async_copy(outer2, new_cache.at[slot], sems.at[slot]).wait()
+
+
+def assemble(ancestors, lengths, new_kv, cache, inner1, outer1):
+    return pl.pallas_call(
+        assemble_kernel,
         out_shape=jax.ShapeDtypeStruct(cache.shape, cache.dtype),
-        in_specs=[SMEM, SMEM, VMEM, ANY, ANY, ANY, ANY, ANY],
-        out_specs=ANY,
+        in_specs=[SMEM, SMEM, VMEM, ANY, ANY, ANY],
+        out_specs=HBM,
         scratch_shapes=[
             pltpu.VMEM(cache.shape, cache.dtype),
-            pltpu.SemaphoreType.DMA((P_DEV, 2, SPLIT)),
-            pltpu.SemaphoreType.DMA((P_DEV, 2, SPLIT)),
+            pltpu.SemaphoreType.DMA((P_DEV, 2)),
+            pltpu.SemaphoreType.DMA((P_DEV, 2)),
         ],
         compiler_params=pltpu.CompilerParams(vmem_limit_bytes=16 << 20),
         name="assemble",
-    )(ancestors, lengths, new_kv, cache, even1, odd1, even2, odd2)
+    )(ancestors, lengths, new_kv, cache, inner1, outer1)
+
+
+def finish(ancestors, inner2, outer2, new_cache, far):
+    return pl.pallas_call(
+        functools.partial(finish_kernel, far),
+        out_shape=jax.ShapeDtypeStruct(new_cache.shape, new_cache.dtype),
+        in_specs=[SMEM, VMEM, VMEM, HBM],
+        out_specs=HBM,
+        input_output_aliases={3: 0},
+        scratch_shapes=[pltpu.SemaphoreType.DMA((P_DEV,))],
+        compiler_params=pltpu.CompilerParams(vmem_limit_bytes=16 << 20),
+        name="finish",
+    )(ancestors, inner2, outer2, new_cache)
 
 
 def normalize_kernel(logits, log_weight):
@@ -452,33 +445,35 @@
 
 
 def local(query, new_kv, cache, lengths, prior_logw, ancestors, w_reward):
-    even0, odd0, rows, flag = pack(ancestors, lengths, query, new_kv, cache)
-    even1 = swapped(even0, "dom", 0)
-    odd1 = swapped(odd0, "dom", 1)
+    inner0, outer0 = pack(ancestors, lengths, new_kv, cache, far=False)
+    inner1 = swapped(inner0, "dom", 0)
+    outer1 = swapped(outer0, "dom", 1)
+    query, outer0 = lax.optimization_barrier((query, outer0))
+    rows, flag = spread(ancestors, query)
     heads = lax.all_to_all(rows, "tp", 0, 0)
+    heads, flag = lax.optimization_barrier((heads, flag))
     parts = attend(lengths, heads, new_kv, cache)
     weight = w_reward.astype(jnp.float32).reshape(HQ, HD)
     sent = parts
     parts = lax.all_to_all(parts, "tp", 0, 0)
-    even1, sent = lax.optimization_barrier((even1, sent))
-    odd2 = swapped(even1, "dom", 1)
-    odd1, sent = lax.optimization_barrier((odd1, sent))
-    even2 = swapped(odd1, "dom", 0)
+    inner1, sent = lax.optimization_barrier((inner1, sent))
+    outer2 = swapped(inner1, "dom", 1)
+    outer1, sent = lax.optimization_barrier((outer1, sent))
+    inner2 = swapped(outer1, "dom", 0)
     attn, logits = merge(prior_logw, parts, weight, query.shape[1], lax.axis_size("dom"))
+    logits, held_ancestors = lax.optimization_barrier((logits, ancestors))
     logits = lax.all_to_all(logits, "dom", 0, 0)
-
-    def near(even2, odd2):
-        return assemble(ancestors, lengths, new_kv, cache, even1, odd1, even2, odd2, far=False)
-
-    def direct(even2, odd2):
-        right0, left0 = pack_far(ancestors, lengths, new_kv, cache)
+    new_cache = assemble(held_ancestors, lengths, new_kv, cache, inner1, outer1)
+
+    new_cache = finish(ancestors, inner2, outer2, new_cache, far=False)
+
+    def direct(new_cache):
+        right0, left0 = pack(ancestors, lengths, new_kv, cache, far=True)
         from_left = shifted(right0, "dom", REACH)
         from_right = shifted(left0, "dom", -REACH)
-        return assemble(
-            ancestors, lengths, new_kv, cache, even1, odd1, from_right, from_left, far=True
-        )
-
-    new_cache = lax.cond(flag[0] > 0, direct, near, even2, odd2)
+        return finish(ancestors, from_right, from_left, new_cache, far=True)
+
+    new_cache = lax.cond(flag[0] > 0, direct, lambda new_cache: new_cache, new_cache)
     new_cache, logits = lax.optimization_barrier((new_cache, logits))
     return (attn, normalize(logits), new_cache)
 

time: 73.9 us -> 71.9 us (0.973)
  the two profiles are of different devices: /device:TPU:46 before, /device:TPU:26 now
where the time goes in v4:
time: 71.9 us; the launch traced here: 71.4 us
  starting transfers between devices  39.4 us (55%)
  Pallas kernels  11.3 us (16%)
  waiting for transfers between devices  10.6 us (15%)
  blocking collectives  8.62 us (12%)
  between operations  1.47 us (2%)
    ppermute x4, starting transfers between devices, swapped(): return lax.ppermute(value, axis, pairs)  23.2 us
    all_to_all x1, starting transfers between devices, local(): logits = lax.all_to_all(logits, 'dom', 0, 0)  11.4 us
    all_to_all x1, blocking collectives, local(): heads = lax.all_to_all(rows, 'tp', 0, 0)  8.62 us
    ppermute x4, waiting for transfers between devices, swapped(): return lax.ppermute(value, axis, pairs)  8.12 us
    all_to_all x1, starting transfers between devices, local(): parts = lax.all_to_all(parts, 'tp', 0, 0)  4.8 us
    pallas_call x1, Pallas kernels, assemble(): pl.pallas_call(assemble_kernel, out_shape=jax.ShapeDtypeStruct(cache.shap...  2.98 us
    all_to_all x1, waiting for transfers between devices, local(): logits = lax.all_to_all(logits, 'dom', 0, 0)  2.44 us
    pallas_call x1, Pallas kernels, pack(): pl.pallas_call(functools.partial(pack_kernel, far), out_shape=(unit, unit...  2.41 us
  transfers between devices with their start and end apart: 6, of which 3 were waited for; matrix products, arithmetic and copies ran while one was open for 0% of the time, Pallas kernels for 11%

profile of v4, /device:TPU:26, one launch (start us, length us, event | category | flops | bytes accessed | tf_op | source)
XLA Modules:
  0.0 71.4 jit_solution(8478264989762310674)
XLA Ops:
  0.6 0.0 copy-start.4
  0.6 0.0 copy-start.6
  0.7 0.0 copy-start.2
  0.7 0.0 copy-start.3
  0.7 0.0 copy-start
  0.7 2.4 %pack.1 = (bf16[2,512,512]{2,1,0:T(8,128)(2,1)S(1)}, bf16[2,512,512]{2,1,0:T(8,128)(2,1)S(1)}) custom-call(s32[128]{0:T(128)} %ancestors.4, s32[2]{0:T(128)} %lengths.5, bf16[2,2,512]{2,1,0:T(2,128)(2,1)} %new_kv.5, bf16[2,2,512,512]{3,2,1,0:T(8,128)(2,1)} %cache.3), custom_call_target="tpu_custom_call" | custom-call | tf_op jit(solution)/shard_map/pack/pallas_call | solution.py:140
  3.1 0.0 copy-start.5
  3.1 0.0 copy-start.1
  3.1 4.3 %collective-permute-start.4 = (bf16[2,512,512]{2,1,0:T(8,128)(2,1)S(1)}, bf16[2,512,512]{2,1,0:T(8,128)(2,1)S(1)}, u32[]{:S(2)}, u32[]{:S(2)}) collective-permute-start(bf16[2,512,512]{2,1,0:T(8,128)(2,1)S(1)} %get-tuple-element.45), channel_id=1, source_target_pairs={{0,8},{8,0},{16,24},{24,16},{32,40},{40,32},{48,56},{56,48},{64,72... | collective-permute-start | bytes 3145736 | tf_op jit(solution)/shard_map/ppermute | solution.py:43
  7.4 9.0 %collective-permute-start.2 = (bf16[2,512,512]{2,1,0:T(8,128)(2,1)S(1)}, bf16[2,512,512]{2,1,0:T(8,128)(2,1)}, u32[]{:S(2)}, u32[]{:S(2)}) collective-permute-start(bf16[2,512,512]{2,1,0:T(8,128)(2,1)S(1)} %get-tuple-element.38), channel_id=1, source_target_pairs={{8,16},{16,8},{24,32},{32,24},{40,48},{48,40},{56,64},{64,56},{72,... | collective-permute-start | bytes 3145736 | tf_op jit(solution)/shard_map/ppermute | solution.py:43
  16.5 0.0 copy-done.4
  16.5 0.0 copy-done
  16.5 0.7 %spread.1 = (f32[8,8,128]{2,1,0:T(8,128)S(1)}, s32[1]{0:T(128)}) custom-call(s32[1,128]{1,0:T(1,128)S(1)} %bitcast.5, bf16[2,448]{1,0:T(2,128)(2,1)S(1)} %copy-done), custom_call_target="tpu_custom_call" | custom-call | tf_op jit(solution)/shard_map/spread/pallas_call | solution.py:98
  17.2 8.6 %all_to_all.15.heads = f32[8,8,128]{2,1,0:T(8,128)S(1)} all-to-all(f32[8,8,128]{2,1,0:T(8,128)S(1)} %get-tuple-element.40), channel_id=1, replica_groups=mesh['dom'=64,'tp'=8] {'tp'}, dimensions={0} | all-to-all | bytes 65536 | tf_op jit(solution)/shard_map/all_to_all | solution.py:453
  25.8 0.0 copy-done.6
  25.8 0.0 copy-done.2
  25.8 0.0 copy-done.3
  25.8 2.2 %attend.1 = f32[8,80,128]{2,1,0:T(8,128)} custom-call(s32[2]{0:T(128)S(1)} %copy-done.6, f32[8,8,128]{2,1,0:T(8,128)S(1)} %all_to_all.15.heads, bf16[2,2,512]{2,1,0:T(2,128)(2,1)S(1)} %copy-done.3, bf16[2,2,512,512]{3,2,1,0:T(8,128)(2,1)S(1)} %copy-done.2), custom_call_target="tpu_custom_call" | custom-call | tf_op jit(solution)/shard_map/attend/pallas_call | solution.py:238
  28.0 4.8 %all-to-all-start.1 = ((f32[8,80,128]{2,1,0:T(8,128)}), f32[8,80,128]{2,1,0:T(8,128)S(1)}, u32[]{:S(2)}, u32[]{:S(2)}) async-start(f32[8,80,128]{2,1,0:T(8,128)} %attend.1), calls=%async_computation.1 | async-start | bytes 655360 | tf_op jit(solution)/shard_map/all_to_all | solution.py:458
  32.8 0.0 copy-done.5
  32.8 0.0 collective-permute-done.4.inner1
  32.8 7.9 %collective-permute-start.5 = (bf16[2,512,512]{2,1,0:T(8,128)(2,1)S(1)}, bf16[2,512,512]{2,1,0:T(8,128)(2,1)S(1)}, u32[]{:S(2)}, u32[]{:S(2)}) collective-permute-start(bf16[2,512,512]{2,1,0:T(8,128)(2,1)S(1)} %collective-permute-done.4.inner1), channel_id=1, source_target_pairs={{8,16},{16,8},{24,32},{32,24},{40,48},{48,40},{56,64},{64,56},{72,... | collective-permute-start | bytes 3145736 | tf_op jit(solution)/shard_map/ppermute | solution.py:43
  40.8 0.0 collective-permute-done.2.outer1
  40.8 1.9 %collective-permute-start.3 = (bf16[2,512,512]{2,1,0:T(8,128)(2,1)}, bf16[2,512,512]{2,1,0:T(8,128)(2,1)S(1)}, u32[]{:S(2)}, u32[]{:S(2)}) collective-permute-start(bf16[2,512,512]{2,1,0:T(8,128)(2,1)} %collective-permute-done.2.outer1), channel_id=1, source_target_pairs={{0,8},{8,0},{16,24},{24,16},{32,40},{40,32},{48,56},{56,48},{64,72... | collective-permute-start | bytes 3145736 | tf_op jit(solution)/shard_map/ppermute | solution.py:43
  42.7 0.0 all-to-all-done.1.parts
  42.7 0.0 copy-done.1
  42.7 1.5 %merge.1 = (bf16[2,448]{1,0:T(2,128)(2,1)}, f32[64,1,128]{2,1,0:T(1,128)}) custom-call(f32[2]{0:T(128)S(1)} %copy-done.1, f32[8,80,128]{2,1,0:T(8,128)S(1)} %all-to-all-done.1.parts, f32[28,128]{1,0:T(8,128)S(1)} %bitcast_convert_fusion.weight), custom_call_target="tpu_custom_call" | custom-call | flops 99999997952 | bytes 1000000000 | tf_op jit(solution)/shard_map/merge/pallas_call | solution.py:303
  44.3 11.4 %all-to-all-start.2 = ((f32[64,1,128]{2,1,0:T(1,128)}), f32[64,1,128]{2,1,0:T(1,128)S(1)}, u32[]{:S(2)}, u32[]{:S(2)}) async-start(f32[64,1,128]{2,1,0:T(1,128)} %get-tuple-element.49), calls=%async_computation.2 | async-start | bytes 65536 | tf_op jit(solution)/shard_map/all_to_all | solution.py:465
  56.3 3.0 %assemble.1.held = bf16[2,2,512,512]{3,2,1,0:T(8,128)(2,1)} custom-call(s32[128]{0:T(128)S(1)} %copy-done.4, s32[2]{0:T(128)S(1)} %copy-done.6, bf16[2,2,512]{2,1,0:T(2,128)(2,1)S(1)} %copy-done.3, bf16[2,2,512,512]{3,2,1,0:T(8,128)(2,1)} %cache.3, bf16[2,512,512]{2,1,0:T(8,128)(2,1)S(1)} %collective-permute-done.4.inner1, ...), custom_call_target="tpu_custom_call" | custom-call | tf_op jit(solution)/shard_map/assemble/pallas_call | solution.py:398
  59.3 4.5 %collective-permute-done.5.outer2 = bf16[2,512,512]{2,1,0:T(8,128)(2,1)S(1)} collective-permute-done((bf16[2,512,512]{2,1,0:T(8,128)(2,1)S(1)}, bf16[2,512,512]{2,1,0:T(8,128)(2,1)S(1)}, u32[]{:S(2)}, u32[]{:S(2)}) %collective-permute-start.5) | collective-permute-done | bytes 1048608 | tf_op jit(solution)/shard_map/ppermute | solution.py:43
  63.8 3.6 %collective-permute-done.3.inner2 = bf16[2,512,512]{2,1,0:T(8,128)(2,1)S(1)} collective-permute-done((bf16[2,512,512]{2,1,0:T(8,128)(2,1)}, bf16[2,512,512]{2,1,0:T(8,128)(2,1)S(1)}, u32[]{:S(2)}, u32[]{:S(2)}) %collective-permute-start.3) | collective-permute-done | bytes 1048608 | tf_op jit(solution)/shard_map/ppermute | solution.py:43
  67.4 0.6 finish.3
  68.0 2.4 %all-to-all-done.2.logits = f32[64,1,128]{2,1,0:T(1,128)S(1)} async-done(((f32[64,1,128]{2,1,0:T(1,128)}), f32[64,1,128]{2,1,0:T(1,128)S(1)}, u32[]{:S(2)}, u32[]{:S(2)}) %all-to-all-start.2) | async-done | bytes 32800 | tf_op jit(solution)/shard_map/all_to_all | solution.py:465
  70.5 0.9 %normalize.1 = f32[2]{0:T(128)} custom-call(f32[64,1,128]{2,1,0:T(1,128)S(1)} %all-to-all-done.2.logits), custom_call_target="tpu_custom_call" | custom-call | tf_op jit(solution)/shard_map/normalize/pallas_call | solution.py:437
  (2 shorter events, 0.0 us)
Async XLA Ops:
  0.6 15.8 %copy-start.4 = (s32[128]{0:T(128)S(1)}, s32[128]{0:T(128)}, u32[]{:S(2)}) copy-start(s32[128]{0:T(128)} %ancestors.4) | copy-start | bytes 1540
  0.6 25.2 %copy-start.6 = (s32[2]{0:T(128)S(1)}, s32[2]{0:T(128)}, u32[]{:S(2)}) copy-start(s32[2]{0:T(128)} %lengths.5) | copy-start | bytes 28
  0.7 25.2 %copy-start.2 = (bf16[2,2,512,512]{3,2,1,0:T(8,128)(2,1)S(1)}, bf16[2,2,512,512]{3,2,1,0:T(8,128)(2,1)}, u32[]{:S(2)}) copy-start(bf16[2,2,512,512]{3,2,1,0:T(8,128)(2,1)} %cache.3) | copy-start | bytes 6291460
  0.7 25.2 %copy-start.3 = (bf16[2,2,512]{2,1,0:T(2,128)(2,1)S(1)}, bf16[2,2,512]{2,1,0:T(2,128)(2,1)}, u32[]{:S(2)}) copy-start(bf16[2,2,512]{2,1,0:T(2,128)(2,1)} %new_kv.5) | copy-start | bytes 12292
  0.7 15.8 %copy-start = (bf16[2,448]{1,0:T(2,128)(2,1)S(1)}, bf16[2,448]{1,0:T(2,128)(2,1)}, u32[]{:S(2)}) copy-start(bf16[2,448]{1,0:T(2,128)(2,1)} %query) | copy-start | bytes 5380
  3.1 29.7 %copy-start.5 = (bf16[3584]{0:T(1024)(128)(2,1)S(1)}, bf16[3584]{0:T(1024)(128)(2,1)}, u32[]{:S(2)}) copy-start(bf16[3584]{0:T(1024)(128)(2,1)} %param.15) | copy-start | bytes 21508
  3.1 39.6 %copy-start.1 = (f32[2]{0:T(128)S(1)}, f32[2]{0:T(128)}, u32[]{:S(2)}) copy-start(f32[2]{0:T(128)} %prior.1) | copy-start | bytes 28
  3.1 29.7 %collective-permute-start.4 = (bf16[2,512,512]{2,1,0:T(8,128)(2,1)S(1)}, bf16[2,512,512]{2,1,0:T(8,128)(2,1)S(1)}, u32[]{:S(2)}, u32[]{:S(2)}) collective-permute-start(bf16[2,512,512]{2,1,0:T(8,128)(2,1)S(1)} %get-tuple-element.45), channel_id=1, source_target_pairs={{0,8},{8,0},{16,24},{24,16},{32,40},{40,32},{48,56},{56,48},{64,72... | collective-permute-start | bytes 3145736 | tf_op jit(solution)/shard_map/ppermute | solution.py:43
  7.4 33.4 %collective-permute-start.2 = (bf16[2,512,512]{2,1,0:T(8,128)(2,1)S(1)}, bf16[2,512,512]{2,1,0:T(8,128)(2,1)}, u32[]{:S(2)}, u32[]{:S(2)}) collective-permute-start(bf16[2,512,512]{2,1,0:T(8,128)(2,1)S(1)} %get-tuple-element.38), channel_id=1, source_target_pairs={{8,16},{16,8},{24,32},{32,24},{40,48},{48,40},{56,64},{64,56},{72,... | collective-permute-start | bytes 3145736 | tf_op jit(solution)/shard_map/ppermute | solution.py:43
  28.0 14.7 %all-to-all-start.1 = ((f32[8,80,128]{2,1,0:T(8,128)}), f32[8,80,128]{2,1,0:T(8,128)S(1)}, u32[]{:S(2)}, u32[]{:S(2)}) async-start(f32[8,80,128]{2,1,0:T(8,128)} %attend.1), calls=%async_computation.1 | async-start | bytes 655360 | tf_op jit(solution)/shard_map/all_to_all | solution.py:458
  32.8 31.0 %collective-permute-start.5 = (bf16[2,512,512]{2,1,0:T(8,128)(2,1)S(1)}, bf16[2,512,512]{2,1,0:T(8,128)(2,1)S(1)}, u32[]{:S(2)}, u32[]{:S(2)}) collective-permute-start(bf16[2,512,512]{2,1,0:T(8,128)(2,1)S(1)} %collective-permute-done.4.inner1), channel_id=1, source_target_pairs={{8,16},{16,8},{24,32},{32,24},{40,48},{48,40},{56,64},{64,56},{72,... | collective-permute-start | bytes 3145736 | tf_op jit(solution)/shard_map/ppermute | solution.py:43
  40.8 26.6 %collective-permute-start.3 = (bf16[2,512,512]{2,1,0:T(8,128)(2,1)}, bf16[2,512,512]{2,1,0:T(8,128)(2,1)S(1)}, u32[]{:S(2)}, u32[]{:S(2)}) collective-permute-start(bf16[2,512,512]{2,1,0:T(8,128)(2,1)} %collective-permute-done.2.outer1), channel_id=1, source_target_pairs={{0,8},{8,0},{16,24},{24,16},{32,40},{40,32},{48,56},{56,48},{64,72... | collective-permute-start | bytes 3145736 | tf_op jit(solution)/shard_map/ppermute | solution.py:43
  44.3 26.2 %all-to-all-start.2 = ((f32[64,1,128]{2,1,0:T(1,128)}), f32[64,1,128]{2,1,0:T(1,128)S(1)}, u32[]{:S(2)}, u32[]{:S(2)}) async-start(f32[64,1,128]{2,1,0:T(1,128)} %get-tuple-element.49), calls=%async_computation.2 | async-start | bytes 65536 | tf_op jit(solution)/shard_map/all_to_all | solution.py:465

commit v5 on v4

--- a/solution.py
+++ b/solution.py
@@ -314,7 +314,6 @@
             pltpu.VMEM((8, OWN * HD), jnp.float32),
         ],
         compiler_params=pltpu.CompilerParams(vmem_limit_bytes=8 << 20),
-        cost_estimate=pl.CostEstimate(flops=10**11, bytes_accessed=10**9, transcendentals=0),
         name="merge",
     )(prior, parts, weight)
 
@@ -454,13 +453,12 @@
     heads, flag = lax.optimization_barrier((heads, flag))
     parts = attend(lengths, heads, new_kv, cache)
     weight = w_reward.astype(jnp.float32).reshape(HQ, HD)
-    sent = parts
     parts = lax.all_to_all(parts, "tp", 0, 0)
-    inner1, sent = lax.optimization_barrier((inner1, sent))
+    attn, logits = merge(prior_logw, parts, weight, query.shape[1], lax.axis_size("dom"))
+    inner1, logits = lax.optimization_barrier((inner1, logits))
     outer2 = swapped(inner1, "dom", 1)
-    outer1, sent = lax.optimization_barrier((outer1, sent))
+    outer1, logits = lax.optimization_barrier((outer1, logits))
     inner2 = swapped(outer1, "dom", 0)
-    attn, logits = merge(prior_logw, parts, weight, query.shape[1], lax.axis_size("dom"))
     logits, held_ancestors = lax.optimization_barrier((logits, ancestors))
     logits = lax.all_to_all(logits, "dom", 0, 0)
     new_cache = assemble(held_ancestors, lengths, new_kv, cache, inner1, outer1)

time: 71.9 us -> 78.6 us (1.093)
  the two profiles are of different devices: /device:TPU:26 before, /device:TPU:6 now
where the time goes in v5:
time: 78.6 us; the launch traced here: 77.5 us
  starting transfers between devices  34.6 us (44%)
  waiting for transfers between devices  19.3 us (25%)
  Pallas kernels  12.9 us (16%)
  blocking collectives  9.23 us (12%)
  between operations  1.44 us (2%)
    all_to_all x1, starting transfers between devices, local(): logits = lax.all_to_all(logits, 'dom', 0, 0)  15.1 us
    ppermute x4, starting transfers between devices, swapped(): return lax.ppermute(value, axis, pairs)  14.1 us
    all_to_all x1, blocking collectives, local(): heads = lax.all_to_all(rows, 'tp', 0, 0)  9.23 us
    all_to_all x1, waiting for transfers between devices, local(): logits = lax.all_to_all(logits, 'dom', 0, 0)  8.25 us
    all_to_all x1, waiting for transfers between devices, local(): parts = lax.all_to_all(parts, 'tp', 0, 0)  6.14 us
    all_to_all x1, starting transfers between devices, local(): parts = lax.all_to_all(parts, 'tp', 0, 0)  5.44 us
    ppermute x4, waiting for transfers between devices, swapped(): return lax.ppermute(value, axis, pairs)  4.89 us
    pallas_call x1, Pallas kernels, pack(): pl.pallas_call(functools.partial(pack_kernel, far), out_shape=(unit, unit...  3.41 us
  transfers between devices with their start and end apart: 6, of which 3 were waited for; matrix products, arithmetic and copies ran while one was open for 0% of the time, Pallas kernels for 11%

profile of v5, /device:TPU:6, one launch (start us, length us, event | category | flops | bytes accessed | tf_op | source)
XLA Modules:
  0.0 77.5 jit_solution(12045538898271454506)
XLA Ops:
  0.6 0.0 copy-start.4
  0.6 0.0 copy-start.6
  0.7 0.0 copy-start.2
  0.7 0.0 copy-start.3
  0.7 0.0 copy-start
  0.7 3.4 %pack.1 = (bf16[2,512,512]{2,1,0:T(8,128)(2,1)}, bf16[2,512,512]{2,1,0:T(8,128)(2,1)S(1)}) custom-call(s32[128]{0:T(128)} %ancestors.4, s32[2]{0:T(128)} %lengths.5, bf16[2,2,512]{2,1,0:T(2,128)(2,1)} %new_kv.5, bf16[2,2,512,512]{3,2,1,0:T(8,128)(2,1)} %cache.3), custom_call_target="tpu_custom_call" | custom-call | tf_op jit(solution)/shard_map/pack/pallas_call | solution.py:140
  4.1 0.0 copy-start.5
  4.1 0.0 copy-start.1
  4.1 4.3 %collective-permute-start.3 = (bf16[2,512,512]{2,1,0:T(8,128)(2,1)}, bf16[2,512,512]{2,1,0:T(8,128)(2,1)S(1)}, u32[]{:S(2)}, u32[]{:S(2)}) collective-permute-start(bf16[2,512,512]{2,1,0:T(8,128)(2,1)} %get-tuple-element.48), channel_id=1, source_target_pairs={{0,8},{8,0},{16,24},{24,16},{32,40},{40,32},{48,56},{56,48},{64,72... | collective-permute-start | bytes 3145736 | tf_op jit(solution)/shard_map/ppermute | solution.py:43
  8.4 1.7 %collective-permute-start.2 = (bf16[2,512,512]{2,1,0:T(8,128)(2,1)S(1)}, bf16[2,512,512]{2,1,0:T(8,128)(2,1)}, u32[]{:S(2)}, u32[]{:S(2)}) collective-permute-start(bf16[2,512,512]{2,1,0:T(8,128)(2,1)S(1)} %get-tuple-element.41), channel_id=1, source_target_pairs={{8,16},{16,8},{24,32},{32,24},{40,48},{48,40},{56,64},{64,56},{72,... | collective-permute-start | bytes 3145736 | tf_op jit(solution)/shard_map/ppermute | solution.py:43
  10.1 0.0 copy-done.4
  10.1 0.0 copy-done
  10.1 0.7 spread.1
  10.8 9.2 %all_to_all.15.heads = f32[8,8,128]{2,1,0:T(8,128)S(1)} all-to-all(f32[8,8,128]{2,1,0:T(8,128)S(1)} %get-tuple-element.43), channel_id=1, replica_groups=mesh['dom'=64,'tp'=8] {'tp'}, dimensions={0} | all-to-all | bytes 65536 | tf_op jit(solution)/shard_map/all_to_all | solution.py:452
  20.0 0.0 copy-done.6
  20.0 0.0 copy-done.2
  20.0 0.0 copy-done.3
  20.1 2.2 %attend.1 = f32[8,80,128]{2,1,0:T(8,128)} custom-call(s32[2]{0:T(128)S(1)} %copy-done.6, f32[8,8,128]{2,1,0:T(8,128)S(1)} %all_to_all.15.heads, bf16[2,2,512]{2,1,0:T(2,128)(2,1)S(1)} %copy-done.3, bf16[2,2,512,512]{3,2,1,0:T(8,128)(2,1)S(1)} %copy-done.2), custom_call_target="tpu_custom_call" | custom-call | tf_op jit(solution)/shard_map/attend/pallas_call | solution.py:238
  22.2 5.4 %all-to-all-start.1 = ((f32[8,80,128]{2,1,0:T(8,128)}), f32[8,80,128]{2,1,0:T(8,128)S(1)}, u32[]{:S(2)}, u32[]{:S(2)}) async-start(f32[8,80,128]{2,1,0:T(8,128)} %attend.1), calls=%async_computation.1 | async-start | bytes 655360 | tf_op jit(solution)/shard_map/all_to_all | solution.py:456
  27.7 0.0 copy-done.5
  27.7 6.1 %all-to-all-done.1.parts = f32[8,80,128]{2,1,0:T(8,128)S(1)} async-done(((f32[8,80,128]{2,1,0:T(8,128)}), f32[8,80,128]{2,1,0:T(8,128)S(1)}, u32[]{:S(2)}, u32[]{:S(2)}) %all-to-all-start.1) | async-done | bytes 327712 | tf_op jit(solution)/shard_map/all_to_all | solution.py:456
  33.8 0.0 copy-done.1
  33.8 1.5 %merge.1 = (bf16[2,448]{1,0:T(2,128)(2,1)}, f32[64,1,128]{2,1,0:T(1,128)}) custom-call(f32[2]{0:T(128)S(1)} %copy-done.1, f32[8,80,128]{2,1,0:T(8,128)S(1)} %all-to-all-done.1.parts, f32[28,128]{1,0:T(8,128)S(1)} %bitcast_convert_fusion.weight), custom_call_target="tpu_custom_call" | custom-call | tf_op jit(solution)/shard_map/merge/pallas_call | solution.py:303
  35.4 0.0 collective-permute-done.3.inner1
  35.4 0.7 collective-permute-start.5
  36.1 0.0 collective-permute-done.2.outer1
  36.1 7.4 %collective-permute-start.4 = (bf16[2,512,512]{2,1,0:T(8,128)(2,1)}, bf16[2,512,512]{2,1,0:T(8,128)(2,1)S(1)}, u32[]{:S(2)}, u32[]{:S(2)}) collective-permute-start(bf16[2,512,512]{2,1,0:T(8,128)(2,1)} %collective-permute-done.2.outer1), channel_id=1, source_target_pairs={{0,8},{8,0},{16,24},{24,16},{32,40},{40,32},{48,56},{56,48},{64,72... | collective-permute-start | bytes 3145736 | tf_op jit(solution)/shard_map/ppermute | solution.py:43
  43.5 15.1 %all-to-all-start.2 = ((f32[64,1,128]{2,1,0:T(1,128)}), f32[64,1,128]{2,1,0:T(1,128)S(1)}, u32[]{:S(2)}, u32[]{:S(2)}) async-start(f32[64,1,128]{2,1,0:T(1,128)} %get-tuple-element.55), calls=%async_computation.2 | async-start | bytes 65536 | tf_op jit(solution)/shard_map/all_to_all | solution.py:463
  59.2 2.6 %assemble.1.held = bf16[2,2,512,512]{3,2,1,0:T(8,128)(2,1)} custom-call(s32[128]{0:T(128)S(1)} %copy-done.4, s32[2]{0:T(128)S(1)} %copy-done.6, bf16[2,2,512]{2,1,0:T(2,128)(2,1)S(1)} %copy-done.3, bf16[2,2,512,512]{3,2,1,0:T(8,128)(2,1)} %cache.3, bf16[2,512,512]{2,1,0:T(8,128)(2,1)S(1)} %collective-permute-done.3.inner1, ...), custom_call_target="tpu_custom_call" | custom-call | tf_op jit(solution)/shard_map/assemble/pallas_call | solution.py:397
  61.9 0.0 collective-permute-done.5.outer2
  61.9 4.9 %collective-permute-done.4.inner2 = bf16[2,512,512]{2,1,0:T(8,128)(2,1)S(1)} collective-permute-done((bf16[2,512,512]{2,1,0:T(8,128)(2,1)}, bf16[2,512,512]{2,1,0:T(8,128)(2,1)S(1)}, u32[]{:S(2)}, u32[]{:S(2)}) %collective-permute-start.4) | collective-permute-done | bytes 1048608 | tf_op jit(solution)/shard_map/ppermute | solution.py:43
  66.8 1.5 %finish.3 = bf16[2,2,512,512]{3,2,1,0:T(8,128)(2,1)} custom-call(s32[128]{0:T(128)S(1)} %copy-done.4, bf16[2,512,512]{2,1,0:T(8,128)(2,1)S(1)} %collective-permute-done.4.inner2, bf16[2,512,512]{2,1,0:T(8,128)(2,1)S(1)} %collective-permute-done.5.outer2, bf16[2,2,512,512]{3,2,1,0:T(8,128)(2,1)} %assemble.1.held), custom_call_target="tpu_custom_call", output_to_operand_aliasing={{}: (3, {})} | custom-call | tf_op jit(solution)/shard_map/finish/pallas_call | solution.py:413
  68.3 8.2 %all-to-all-done.2.logits = f32[64,1,128]{2,1,0:T(1,128)S(1)} async-done(((f32[64,1,128]{2,1,0:T(1,128)}), f32[64,1,128]{2,1,0:T(1,128)S(1)}, u32[]{:S(2)}, u32[]{:S(2)}) %all-to-all-start.2) | async-done | bytes 32800 | tf_op jit(solution)/shard_map/all_to_all | solution.py:463
  76.6 0.9 %normalize.1 = f32[2]{0:T(128)} custom-call(f32[64,1,128]{2,1,0:T(1,128)S(1)} %all-to-all-done.2.logits), custom_call_target="tpu_custom_call" | custom-call | tf_op jit(solution)/shard_map/normalize/pallas_call | solution.py:436
  (2 shorter events, 0.0 us)
Async XLA Ops:
  0.6 9.5 %copy-start.4 = (s32[128]{0:T(128)S(1)}, s32[128]{0:T(128)}, u32[]{:S(2)}) copy-start(s32[128]{0:T(128)} %ancestors.4) | copy-start | bytes 1540
  0.6 19.4 %copy-start.6 = (s32[2]{0:T(128)S(1)}, s32[2]{0:T(128)}, u32[]{:S(2)}) copy-start(s32[2]{0:T(128)} %lengths.5) | copy-start | bytes 28
  0.7 19.4 %copy-start.2 = (bf16[2,2,512,512]{3,2,1,0:T(8,128)(2,1)S(1)}, bf16[2,2,512,512]{3,2,1,0:T(8,128)(2,1)}, u32[]{:S(2)}) copy-start(bf16[2,2,512,512]{3,2,1,0:T(8,128)(2,1)} %cache.3) | copy-start | bytes 6291460
  0.7 19.4 %copy-start.3 = (bf16[2,2,512]{2,1,0:T(2,128)(2,1)S(1)}, bf16[2,2,512]{2,1,0:T(2,128)(2,1)}, u32[]{:S(2)}) copy-start(bf16[2,2,512]{2,1,0:T(2,128)(2,1)} %new_kv.5) | copy-start | bytes 12292
  0.7 9.4 %copy-start = (bf16[2,448]{1,0:T(2,128)(2,1)S(1)}, bf16[2,448]{1,0:T(2,128)(2,1)}, u32[]{:S(2)}) copy-start(bf16[2,448]{1,0:T(2,128)(2,1)} %query) | copy-start | bytes 5380
  4.1 23.6 %copy-start.5 = (bf16[3584]{0:T(1024)(128)(2,1)S(1)}, bf16[3584]{0:T(1024)(128)(2,1)}, u32[]{:S(2)}) copy-start(bf16[3584]{0:T(1024)(128)(2,1)} %param.15) | copy-start | bytes 21508
  4.1 29.7 %copy-start.1 = (f32[2]{0:T(128)S(1)}, f32[2]{0:T(128)}, u32[]{:S(2)}) copy-start(f32[2]{0:T(128)} %prior.1) | copy-start | bytes 28
  4.1 31.3 %collective-permute-start.3 = (bf16[2,512,512]{2,1,0:T(8,128)(2,1)}, bf16[2,512,512]{2,1,0:T(8,128)(2,1)S(1)}, u32[]{:S(2)}, u32[]{:S(2)}) collective-permute-start(bf16[2,512,512]{2,1,0:T(8,128)(2,1)} %get-tuple-element.48), channel_id=1, source_target_pairs={{0,8},{8,0},{16,24},{24,16},{32,40},{40,32},{48,56},{56,48},{64,72... | collective-permute-start | bytes 3145736 | tf_op jit(solution)/shard_map/ppermute | solution.py:43
  8.4 27.7 %collective-permute-start.2 = (bf16[2,512,512]{2,1,0:T(8,128)(2,1)S(1)}, bf16[2,512,512]{2,1,0:T(8,128)(2,1)}, u32[]{:S(2)}, u32[]{:S(2)}) collective-permute-start(bf16[2,512,512]{2,1,0:T(8,128)(2,1)S(1)} %get-tuple-element.41), channel_id=1, source_target_pairs={{8,16},{16,8},{24,32},{32,24},{40,48},{48,40},{56,64},{64,56},{72,... | collective-permute-start | bytes 3145736 | tf_op jit(solution)/shard_map/ppermute | solution.py:43
  22.2 11.6 %all-to-all-start.1 = ((f32[8,80,128]{2,1,0:T(8,128)}), f32[8,80,128]{2,1,0:T(8,128)S(1)}, u32[]{:S(2)}, u32[]{:S(2)}) async-start(f32[8,80,128]{2,1,0:T(8,128)} %attend.1), calls=%async_computation.1 | async-start | bytes 655360 | tf_op jit(solution)/shard_map/all_to_all | solution.py:456
  35.4 26.5 %collective-permute-start.5 = (bf16[2,512,512]{2,1,0:T(8,128)(2,1)S(1)}, bf16[2,512,512]{2,1,0:T(8,128)(2,1)S(1)}, u32[]{:S(2)}, u32[]{:S(2)}) collective-permute-start(bf16[2,512,512]{2,1,0:T(8,128)(2,1)S(1)} %collective-permute-done.3.inner1), channel_id=1, source_target_pairs={{8,16},{16,8},{24,32},{32,24},{40,48},{48,40},{56,64},{64,56},{72,... | collective-permute-start | bytes 3145736 | tf_op jit(solution)/shard_map/ppermute | solution.py:43
  36.1 30.6 %collective-permute-start.4 = (bf16[2,512,512]{2,1,0:T(8,128)(2,1)}, bf16[2,512,512]{2,1,0:T(8,128)(2,1)S(1)}, u32[]{:S(2)}, u32[]{:S(2)}) collective-permute-start(bf16[2,512,512]{2,1,0:T(8,128)(2,1)} %collective-permute-done.2.outer1), channel_id=1, source_target_pairs={{0,8},{8,0},{16,24},{24,16},{32,40},{40,32},{48,56},{56,48},{64,72... | collective-permute-start | bytes 3145736 | tf_op jit(solution)/shard_map/ppermute | solution.py:43
  43.5 33.1 %all-to-all-start.2 = ((f32[64,1,128]{2,1,0:T(1,128)}), f32[64,1,128]{2,1,0:T(1,128)S(1)}, u32[]{:S(2)}, u32[]{:S(2)}) async-start(f32[64,1,128]{2,1,0:T(1,128)} %get-tuple-element.55), calls=%async_computation.2 | async-start | bytes 65536 | tf_op jit(solution)/shard_map/all_to_all | solution.py:463
